TPU v7x, 512 devices: a whole 4x8x8 slice. The times are simulated.
512 devices in a mesh: dp: 4 (over x), fsdp: 128 (over z, y, core).
Axes of the slice: x: 4, y: 8, z: 8, core: 2. Of those that a mesh axis runs over, the one named last changes fastest.
Arguments:
- gradient: bfloat16 [4, 8, 512, 8192], P('dp', None, 'fsdp'), may hold values from -6 to 6
- owner_slot: int32 [8, 16], replicated, may hold values from 0 to 255, as said below
- stat_left: float32 [256, 512, 512], P('fsdp', 'dp'), may hold values from -12 to 12
- stat_right: float32 [256, 512, 512], P('fsdp', 'dp'), may hold values from -12 to 12
- second_moment: float32 [256, 512, 512], P('fsdp', 'dp'), may hold values from 0.05 to 1
- basis_left: bfloat16 [256, 512, 512], P('fsdp', None, 'dp'), may hold values from -0.25 to 0.25
- basis_right: bfloat16 [256, 512, 512], P('fsdp', 'dp'), may hold values from -0.25 to 0.25
Outputs:
- update: bfloat16 [8, 512, 16, 512], P(None, 'fsdp', None, 'dp')
- new_left: float32 [256, 512, 512], P('fsdp', 'dp')
- new_right: float32 [256, 512, 512], P('fsdp', 'dp')
- new_moment: float32 [256, 512, 512], P('fsdp', 'dp')
Inputs may be any that keep to these rules, and one draw needn't show every extreme that they name: `owner_slot`: 128 distinct slot numbers; slot s belongs to fsdp index s // 2. A quarter of the fsdp indices, always including the first and the last, own 2 blocks, half own 1, a quarter own none; which slots of an index are used is drawn from the seed.
All inputs are finite; a program needn't handle non-finite values.
Results may differ from a plain program's by a relative error of at most 0.022.
Values may be sent and summed in bfloat16 or wider, within the bound.
A program may use at most 64 MiB of HBM per device.

v0:
```python
import jax
import jax.numpy as jnp
from jax import lax
from jax.sharding import PartitionSpec as P

epsilon = 1e-08


def local(gradient, owner_slot, stat_left, stat_right, second_moment, basis_left, basis_right):
    groups = lax.axis_size("dp")
    dp_place = lax.axis_index("dp")
    owner_index = lax.axis_index("fsdp")
    local_grad = gradient[0]
    layers, row_dev, columns = local_grad.shape
    capacity = stat_left.shape[0]
    order_b = basis_right.shape[2]
    quarter = order_b // groups
    blocks_per = columns // order_b
    slot_count = capacity * lax.axis_size("fsdp")
    slot_flat = owner_slot.reshape(-1)
    pieces = local_grad.reshape(layers, row_dev, blocks_per, order_b)
    pieces = jnp.transpose(pieces, (0, 2, 1, 3)).reshape(layers * blocks_per, row_dev, order_b)
    filled = jnp.zeros((slot_count,) + pieces.shape[1:], pieces.dtype).at[slot_flat].set(pieces)
    owned = lax.all_to_all(filled, "fsdp", split_axis=0, concat_axis=1, tiled=True)
    summed = lax.psum(owned.astype(jnp.float32).astype(jnp.bfloat16), "dp").astype(jnp.float32)
    owned_block = (summed / groups).astype(jnp.bfloat16)
    slot_marks = jnp.zeros((slot_count,), jnp.int32).at[slot_flat].set(1)
    in_use = (lax.dynamic_slice_in_dim(slot_marks, owner_index * capacity, capacity) > 0)[
        :, None, None
    ]
    right_full = lax.all_gather(basis_right, "dp", axis=1, tiled=True)
    block_rows = lax.dynamic_slice_in_dim(owned_block, dp_place * quarter, quarter, 1)
    block_cols = lax.dynamic_slice_in_dim(owned_block, dp_place * quarter, quarter, 2)
    left_term = jnp.einsum(
        "sqj,skj->sqk", block_rows, owned_block, preferred_element_type=jnp.float32
    )
    right_term = jnp.einsum(
        "siq,sij->sqj", block_cols, owned_block, preferred_element_type=jnp.float32
    )
    new_left = jnp.where(in_use, 0.95 * stat_left + 0.05 * left_term, stat_left)
    new_right = jnp.where(in_use, 0.95 * stat_right + 0.05 * right_term, stat_right)
    half_turn = jnp.einsum(
        "siq,sij->sqj", basis_left, owned_block, preferred_element_type=jnp.float32
    ).astype(jnp.bfloat16)
    rotated = jnp.einsum("sqj,sjk->sqk", half_turn, right_full, preferred_element_type=jnp.float32)
    moment = 0.95 * second_moment + 0.05 * rotated * rotated
    new_moment = jnp.where(in_use, moment, second_moment)
    scaled = (rotated / (jnp.sqrt(moment) + epsilon)).astype(jnp.bfloat16)
    back_turn = jnp.einsum(
        "sqj,skj->sqk", scaled, right_full, preferred_element_type=jnp.float32
    ).astype(jnp.bfloat16)
    partial_value = jnp.einsum(
        "siq,sqk->sik", basis_left, back_turn, preferred_element_type=jnp.float32
    )
    mixed = lax.psum_scatter(
        partial_value.astype(jnp.bfloat16), "dp", scatter_dimension=2, tiled=True
    )
    returned = lax.all_to_all(mixed, "fsdp", split_axis=1, concat_axis=0, tiled=True)
    picked = jnp.take(returned, slot_flat, axis=0)
    update = jnp.transpose(picked.reshape(layers, blocks_per, row_dev, quarter), (0, 2, 1, 3))
    return (update, new_left, new_right, new_moment)


def solution(mesh):
    placed = (
        P("dp", None, "fsdp", None),
        P(),
        P("fsdp", "dp", None),
        P("fsdp", "dp", None),
        P("fsdp", "dp", None),
        P("fsdp", None, "dp"),
        P("fsdp", "dp", None),
    )
    return jax.shard_map(
        local,
        mesh=mesh,
        in_specs=placed,
        out_specs=(
            P(None, "fsdp", None, "dp"),
            P("fsdp", "dp", None),
            P("fsdp", "dp", None),
            P("fsdp", "dp", None),
        ),
        check_vma=False,
    )
```

profile of v0, /device:TPU:1, one launch (start us, length us, event | category | flops | bytes accessed | tf_op | source)
XLA Modules:
  0.0 211.1 jit_solution(13091100679951735924)
XLA Ops:
  7.2 0.0 copy-start
  7.2 0.8 reshape.52
  8.0 1.4 reshape.78
  9.5 0.4 copy.46
  9.9 1.2 broadcast_in_dim.37
  11.1 14.4 %scatter_fusion = bf16[256,4,512]{2,1,0:T(4,128)(2,1)} fusion(bf16[256,4,512]{2,1,0:T(4,128)(2,1)} %broadcast_in_dim.37, s32[128]{0:T(128)S(1)} %fusion.16, bf16[128,4,512]{2,1,0:T(4,128)(2,1)S(1)} %copy.46), kind=kCustom, calls=%fused_computation.1 | custom fusion | bytes 1573376 | tf_op jit(solution)/shard_map/scatter | solution.py:23
  25.6 18.4 %all-to-all-start = ((bf16[256,4,512]{2,1,0:T(4,128)(2,1)}), bf16[256,4,512]{2,1,0:T(4,128)(2,1)S(1)}, u32[]{:S(2)}, u32[]{:S(2)}) async-start(bf16[256,4,512]{2,1,0:T(4,128)(2,1)} %scatter_fusion), calls=%async_computation | async-start | bytes 2097152 | tf_op jit(solution)/shard_map/all_to_all | solution.py:24
  44.0 0.0 all-gather.2.cloned.1.call-start
  44.0 0.7 all-gather.2.cloned.1.call-update
  44.7 0.0 all-reduce.2.cloned.1.call-start
  44.8 30.1 %all-to-all-done = bf16[256,4,512]{2,1,0:T(4,128)(2,1)S(1)} async-done(((bf16[256,4,512]{2,1,0:T(4,128)(2,1)}), bf16[256,4,512]{2,1,0:T(4,128)(2,1)S(1)}, u32[]{:S(2)}, u32[]{:S(2)}) %all-to-all-start) | async-done | bytes 1048608 | tf_op jit(solution)/shard_map/all_to_all | solution.py:24
  74.9 0.8 copy.47
  75.7 2.5 %copy.48 = bf16[2,512,512]{1,2,0:T(8,128)(2,1)} copy(bf16[2,512,512]{2,0,1:T(2,128)(2,1)S(1)} %bitcast.25) | data formatting | bytes 2097152 | tf_op jit(solution)/shard_map/all_to_all | solution.py:24
  78.2 0.0 copy-start.3
  78.2 0.0 all-reduce.2.cloned.1.call-update
  78.2 0.0 reduce-scatter.2.cloned.1.call-start
  78.3 1.0 scatter_custom_fusion.1
  79.3 0.1 dynamic-slice_compare_fusion
  79.4 0.0 all-gather.2.cloned.1.call-done
  79.4 0.0 copy-start.2
  79.4 55.6 %all-reduce.2.cloned.1.call-done = bf16[2,512,512]{1,2,0:T(8,128)(2,1)} async-done(((bf16[2,512,512]{1,2,0:T(8,128)(2,1)}), bf16[2,512,512]{1,2,0:T(8,128)(2,1)}) %all-reduce.2.cloned.1.call-update) | async-done | bytes 1048592 | tf_op jit(solution)/shard_map/psum | solution.py:25
  134.9 0.0 copy-done
  134.9 0.0 copy-done.3
  134.9 3.1 %fusion.7 = (f32[2,128,512]{2,1,0:T(8,128)}, f32[2,128,512]{2,1,0:T(8,128)S(1)}) fusion(f32[2,128,512]{2,1,0:T(8,128)S(1)} %copy-done.3, pred[2]{0:T(512)(128)(4,1)S(1)} %dynamic-slice_compare_fusion, bf16[2,512,512]{2,1,0:T(8,128)(2,1)} %all-gather.2.cloned.1.call-done, bf16[2,512,128]{2,1,0:T(8,128)(2,1)S(1)} %copy-done, ...), kind=kOutput, calls=%fused_computation.18 | convolution fusion | flops 270794752 | bytes 3932162 | tf_op jit(solution)/shard_map/sqj,sjk->sqk/dot_general | solution.py:45
  138.0 0.0 copy-done.2
  138.0 1.8 fusion
  139.8 0.0 copy-start.6
  139.8 0.0 copy-start.1
  139.8 0.0 reduce-scatter.2.cloned.1.call-update
  139.9 0.6 copy-done.6
  140.5 0.5 copy-done.1
  141.0 0.2 multiply_convert_fusion
  141.2 0.0 copy-start.4
  141.3 28.4 %reduce-scatter.2.cloned.1.call-done = bf16[2,512,128]{1,2,0:T(8,128)(2,1)} async-done(((bf16[2,512,512]{1,2,0:T(8,128)(2,1)}), bf16[2,512,128]{1,2,0:T(8,128)(2,1)}) %reduce-scatter.2.cloned.1.call-update) | async-done | bytes 262160 | tf_op jit(solution)/shard_map/reduce_scatter | solution.py:55
  169.7 1.8 copy.51
  171.5 15.7 %all-to-all-start.1 = ((bf16[2,512,128]{2,0,1:T(2,128)(2,1)}), bf16[2,512,128]{2,0,1:T(2,128)(2,1)S(1)}, u32[]{:S(2)}, u32[]{:S(2)}) async-start(bf16[2,512,128]{2,0,1:T(2,128)(2,1)} %copy.51), calls=%async_computation.2 | async-start | bytes 524288 | tf_op jit(solution)/shard_map/all_to_all | solution.py:58
  187.2 0.0 copy-done.4
  187.3 0.0 copy-start.5
  187.3 1.2 fusion.2
  188.4 0.0 copy-done.5
  188.4 1.3 fusion.4
  189.7 12.8 %all-to-all-done.1 = bf16[2,512,128]{2,0,1:T(2,128)(2,1)S(1)} async-done(((bf16[2,512,128]{2,0,1:T(2,128)(2,1)}), bf16[2,512,128]{2,0,1:T(2,128)(2,1)S(1)}, u32[]{:S(2)}, u32[]{:S(2)}) %all-to-all-start.1) | async-done | bytes 262176 | tf_op jit(solution)/shard_map/all_to_all | solution.py:58
  202.5 0.3 copy.53
  202.8 0.2 copy.54
  203.0 0.7 gather_fusion
  203.8 0.1 select_bitcast_fusion
  203.9 0.7 copy.59
  (7 shorter events, 0.1 us)
Async XLA Ops:
  7.2 127.8 %copy-start = (bf16[2,512,128]{2,1,0:T(8,128)(2,1)S(1)}, bf16[2,512,128]{2,1,0:T(8,128)(2,1)}, u32[]{:S(2)}) copy-start(bf16[2,512,128]{2,1,0:T(8,128)(2,1)} %param.12) | copy-start | bytes 786436
  25.6 49.3 %all-to-all-start = ((bf16[256,4,512]{2,1,0:T(4,128)(2,1)}), bf16[256,4,512]{2,1,0:T(4,128)(2,1)S(1)}, u32[]{:S(2)}, u32[]{:S(2)}) async-start(bf16[256,4,512]{2,1,0:T(4,128)(2,1)} %scatter_fusion), calls=%async_computation | async-start | bytes 2097152 | tf_op jit(solution)/shard_map/all_to_all | solution.py:24
  44.0 35.4 %all-gather.2.cloned.1.call-start = ((), (), s32[]{:S(2)}) async-start(), calls=%async_computation.4 | async-start | bytes 1310720 | tf_op jit(solution)/shard_map/all_gather | solution.py:31
  44.7 90.2 %all-reduce.2.cloned.1.call-start = ((), (), s32[]{:S(2)}) async-start(), calls=%async_computation.3 | async-start | bytes 2097152 | tf_op jit(solution)/shard_map/psum | solution.py:25
  78.2 56.7 %copy-start.3 = (f32[2,128,512]{2,1,0:T(8,128)S(1)}, f32[2,128,512]{2,1,0:T(8,128)}, u32[]{:S(2)}) copy-start(f32[2,128,512]{2,1,0:T(8,128)} %param.11) | copy-start | bytes 1572868
  78.2 91.5 %reduce-scatter.2.cloned.1.call-start = ((), (), s32[]{:S(2)}) async-start(), calls=%async_computation.5 | async-start | bytes 1310720 | tf_op jit(solution)/shard_map/reduce_scatter | solution.py:55
  79.4 58.7 %copy-start.2 = (bf16[2,512,512]{2,1,0:T(8,128)(2,1)S(1)}, bf16[2,512,512]{2,1,0:T(8,128)(2,1)}, u32[]{:S(2)}) copy-start(bf16[2,512,512]{2,1,0:T(8,128)(2,1)} %all-gather.2.cloned.1.call-done) | copy-start | bytes 3145732
  139.8 0.7 copy-start.6
  139.8 1.2 copy-start.1
  141.2 46.0 %copy-start.4 = (f32[2,128,512]{2,1,0:T(8,128)S(1)}, f32[2,128,512]{2,1,0:T(8,128)}, u32[]{:S(2)}) copy-start(f32[2,128,512]{2,1,0:T(8,128)} %param.9) | copy-start | bytes 1572868
  171.5 31.0 %all-to-all-start.1 = ((bf16[2,512,128]{2,0,1:T(2,128)(2,1)}), bf16[2,512,128]{2,0,1:T(2,128)(2,1)S(1)}, u32[]{:S(2)}, u32[]{:S(2)}) async-start(bf16[2,512,128]{2,0,1:T(2,128)(2,1)} %copy.51), calls=%async_computation.2 | async-start | bytes 524288 | tf_op jit(solution)/shard_map/all_to_all | solution.py:58
  187.3 1.2 copy-start.5
Sparse Core Ops, SparseCore 0:
  46.9 29.1 all-gather.1
  78.5 56.4 all-reduce.1
  140.0 29.6 reduce-scatter.1
where the time goes:
time: 212 us; the launch traced here: 211 us
  waiting for transfers between devices  128 us (60%)
  starting transfers between devices  34.3 us (16%)
  local copies, waits for them, and re-layouts  27.6 us (13%)
  between operations  13.9 us (7%)
  matrix products  7.29 us (3%)
    psum x1, waiting for transfers between devices, local(): lax.psum(owned.astype(jnp.float32).astype(jnp.bfloat16), 'dp')  55.6 us
    all_to_all x1, waiting for transfers between devices, local(): lax.all_to_all(filled, 'fsdp', split_axis=0, concat_axis=1, tiled=True)  30.1 us
    reduce_scatter x1, waiting for transfers between devices, local(): lax.psum_scatter(partial_value.astype(jnp.bfloat16), 'dp', scatter_dimens...  28.4 us
    all_to_all x1, starting transfers between devices, local(): lax.all_to_all(filled, 'fsdp', split_axis=0, concat_axis=1, tiled=True)  18.4 us
    all_to_all x1, starting transfers between devices, local(): lax.all_to_all(mixed, 'fsdp', split_axis=1, concat_axis=0, tiled=True)  15.7 us
    scatter x1, local copies, waits for them, and re-layouts, local(): jnp.zeros((slot_count,) + pieces.shape[1:], pieces.dtype).at[slot_flat]  14.4 us
    all_to_all x1, waiting for transfers between devices, local(): lax.all_to_all(mixed, 'fsdp', split_axis=1, concat_axis=0, tiled=True)  12.8 us
  transfers between devices with their start and end apart: 5, of which 4 were waited for; matrix products, arithmetic and copies ran while one was open for 3% of the time, Pallas kernels for 0%

commit v1 on v0

v1 whole, which is shorter than its diff:
```python
import functools

import jax
import jax.numpy as jnp
from jax import lax
from jax.experimental import pallas as pl
from jax.experimental.pallas import tpu as pltpu
from jax.sharding import PartitionSpec as P

epsilon = 1e-08
MESH = pl.DeviceIdType.MESH
F32, BF16, I32 = jnp.float32, jnp.bfloat16, jnp.int32
LINE = 8
LANES = 128


def iota(shape, dim):
    return lax.broadcasted_iota(I32, shape, dim)


def dot(a, b, ca=1, cb=0):
    return lax.dot_general(a, b, (((ca,), (cb,)), ((), ())), preferred_element_type=F32)


def one_hot(rows, columns):
    return jnp.where(rows == columns, 1.0, 0.0).astype(BF16)


def kernel(
    slot_ref, grad_ref, left_ref, right_ref, moment_ref, bl_ref, br_ref,
    update_ref, new_left_ref, new_right_ref, new_moment_ref,
    raw, mean, pick, place, sort_in, sort_out,
    send_b, recv_b, g_full, l_full, r_full, l_own, back_own, back_full,
    out_own, out_send, out_recv, send_e, recv_e, stat_l, stat_r, stat_m,
    local_sem, a_send, a_recv, x_send, x_recv, b_send, b_recv, c_send, c_recv,
    l_send, l_recv, r_send, r_recv, d_send, d_recv, y_send, y_recv, e_send, e_recv, ready,
):
    x = lax.axis_index("dp")
    f = lax.axis_index("fsdp")
    groups = 4
    core = lax.rem(f, 2)
    chip = f // 2
    z, y = chip // LINE, lax.rem(chip, LINE)
    chips = LINE * LINE
    sibling = (x, f + 1 - 2 * core)
    layers, rows, blocks_per, _ = grad_ref.shape
    order = g_full.shape[1]

    def x_peer(d):
        return lax.rem(x + d, groups)

    def device(zz, yy):
        return (x, (zz * LINE + yy) * 2 + core)

    def z_peer(d):
        return device(lax.rem(z + d, LINE), y)

    def y_peer(d):
        return device(z, lax.rem(y + d, LINE))

    def column(p):
        return pl.ds(pl.multiple_of(p * LANES, LANES), LANES)

    def remote(src, dst, send, recv, to):
        return pltpu.make_async_remote_copy(
            src_ref=src, dst_ref=dst, send_sem=send, recv_sem=recv,
            device_id=to, device_id_type=MESH,
        )

    def arrived(ref, sem):
        pltpu.make_async_copy(ref, ref, sem).wait()

    loads = [
        pltpu.make_async_copy(grad_ref.at[:, :, :, column(x)], raw.at[3], local_sem.at[0]),
        pltpu.make_async_copy(bl_ref, l_own, local_sem.at[1]),
        pltpu.make_async_copy(left_ref, stat_l, local_sem.at[2]),
        pltpu.make_async_copy(right_ref, stat_r, local_sem.at[3]),
        pltpu.make_async_copy(moment_ref, stat_m, local_sem.at[4]),
    ]
    for t in range(2):
        loads.append(pltpu.make_async_copy(bl_ref.at[t], l_full.at[t, :, column(x)], local_sem.at[5 + t]))
        loads.append(pltpu.make_async_copy(br_ref.at[t], r_full.at[t, column(x), :], local_sem.at[7 + t]))
    for load in loads:
        load.start()

    barrier = pltpu.get_barrier_semaphore()
    for d in range(1, groups):
        pl.semaphore_signal(barrier, inc=1, device_id=(x_peer(d), f), device_id_type=MESH)
    pl.semaphore_signal(barrier, inc=1, device_id=sibling, device_id_type=MESH)
    for d in range(1, LINE):
        pl.semaphore_signal(barrier, inc=1, device_id=z_peer(d), device_id_type=MESH)
        pl.semaphore_signal(barrier, inc=1, device_id=y_peer(d), device_id_type=MESH)
    pl.semaphore_wait(barrier, groups + 2 * (LINE - 1))

    for d in range(1, groups):
        p = x_peer(d)
        remote(grad_ref.at[:, :, :, column(p)], raw.at[d - 1], a_send, a_recv, (p, f)).start()
    for d in range(1, LINE):
        pl.semaphore_signal(ready, inc=1, device_id=y_peer(d), device_id_type=MESH)

    many = layers * rows * blocks_per
    slots = slot_ref[...].astype(F32).astype(BF16)
    spread = one_hot(lax.rem(iota((blocks_per, many), 1), blocks_per), iota((blocks_per, many), 0))
    wide = dot(slots, spread)
    own_layer = iota((layers, many), 1) // (rows * blocks_per) == iota((layers, many), 0)
    slot_lane = jnp.sum(jnp.where(own_layer, wide, 0.0), axis=0, keepdims=True).astype(I32)
    row_lane = lax.rem(iota((1, many), 1) // blocks_per, rows)
    owner_lane = slot_lane // 2
    code_lane = jnp.where(
        lax.rem(owner_lane, 2) == core,
        (owner_lane // 2) * 2 * rows + lax.rem(slot_lane, 2) * rows + row_lane, -1,
    )
    used = [jnp.max(jnp.where(slot_lane == 2 * f + t, 1.0, 0.0), axis=1, keepdims=True) for t in range(2)]
    pick[...] = one_hot(code_lane, iota((chips * 2 * rows, many), 0))
    tall_spread = one_hot(lax.rem(iota((many, blocks_per), 0), blocks_per), iota((many, blocks_per), 1))
    tall = dot(tall_spread, slots, 1, 1)
    tall_layer = iota((many, layers), 0) // (rows * blocks_per) == iota((many, layers), 1)
    slot_col = jnp.sum(jnp.where(tall_layer, tall, 0.0), axis=1, keepdims=True).astype(I32)
    row_col = lax.rem(iota((many, 1), 0) // blocks_per, rows)
    owner_col = slot_col // 2
    far = jnp.where(lax.rem(owner_col, 2) == core, 0, 1)
    code_col = ((owner_col // 2) * 2 + far) * 2 * rows + lax.rem(slot_col, 2) * rows + row_col
    place[...] = one_hot(code_col, iota((many, chips * 4 * rows), 1))
    chunk = 256
    per = chunk // (4 * rows)
    ro, co = iota((chunk, 1), 0), iota((1, chunk), 1)
    far_o = lax.rem(lax.rem(ro // rows, 2) + core, 2)
    want = ((lax.rem(ro // (2 * rows), per) * 2 + far_o) * 2 + ro // (chunk // 2)) * rows + lax.rem(ro, rows)
    sort_in[...] = one_hot(want, co)
    core_o = lax.rem(ro // (chunk // 2) + core, 2)
    chip_o = lax.rem(ro // (2 * rows), per)
    t_o = lax.rem(ro // rows, 2)
    want = ((t_o * per + chip_o) * 2 + core_o) * rows + lax.rem(ro, rows)
    sort_out[...] = one_hot(want, co)

    loads[0].wait()
    arrived(raw.at[pl.ds(0, 3)], a_recv)
    for load in loads[1:]:
        load.wait()
    total = raw[0].astype(F32) + raw[1].astype(F32) + raw[2].astype(F32) + raw[3].astype(F32)
    mean[0] = (total * (1.0 / groups)).astype(BF16).reshape(many, LANES)
    share = remote(mean.at[0], mean.at[1], x_send, x_recv, sibling)
    share.start()
    for d in range(1, groups):
        for t in range(2):
            remote(br_ref.at[t], r_full.at[t, column(x), :], r_send, r_recv, (x_peer(d), f)).start()
    for d in range(1, groups):
        for t in range(2):
            remote(bl_ref.at[t], l_full.at[t, :, column(x)], l_send, l_recv, (x_peer(d), f)).start()
    near = dot(pick[...], mean[0]).reshape(chips, 2 * rows, LANES)
    share.wait()
    away = dot(pick[...], mean[1]).reshape(chips, 2 * rows, LANES)
    send_b[...] = jnp.concatenate([near, away], axis=1).astype(BF16)

    pl.semaphore_wait(ready, LINE - 1)

    def all_to_all(src, dst, send, recv):
        def step(i, carry):
            to = lax.rem(chip + i * 37, chips)
            remote(src.at[to], dst.at[chip], send, recv, (x, to * 2 + core)).start()
            return carry
        lax.fori_loop(1, chips, step, 0)
        dst[chip] = src[chip]
        arrived(dst.at[pl.ds(0, chips - 1)], recv)

    all_to_all(send_b, recv_b, b_send, b_recv)
    for j in range(chips // per):
        part = dot(sort_in[...], recv_b[j * per : (j + 1) * per].reshape(chunk, LANES)).astype(BF16)
        half = chunk // 2
        for t in range(2):
            g_full[t, j * half : (j + 1) * half, column(x)] = part[t * half : (t + 1) * half]
    for t in range(2):
        for d in range(1, groups):
            mine = g_full.at[t, :, column(x)]
            remote(mine, mine, c_send, c_recv.at[t], (x_peer(d), f)).start()
    quarter = order // groups
    parts = pl.ds(0, order - quarter)
    for t in range(2):
        arrived(g_full.at[t, parts, :], c_recv.at[t])
        if t == 0:
            arrived(r_full.at[:, parts, :], r_recv)
        block = g_full[t]
        right = r_full[t]
        half_turn = dot(l_own[t], block, 0, 0).astype(BF16)
        rotated = dot(half_turn, right)
        moment = 0.95 * stat_m[t] + 0.05 * rotated * rotated
        new_moment_ref[t] = jnp.where(used[t] > 0.0, moment, stat_m[t])
        scaled = (rotated / (jnp.sqrt(moment) + epsilon)).astype(BF16)
        back_own[t] = dot(scaled, right, 1, 1).astype(BF16)
        for d in range(1, groups):
            p = x_peer(d)
            remote(
                back_own.at[t, :, column(p)], back_full.at[t, column(x), :],
                d_send, d_recv.at[t], (p, f),
            ).start()
        back_full[t, column(x), :] = back_own[t, :, column(x)]
    arrived(l_full.at[:, parts, :], l_recv)
    outs = []
    for t in range(2):
        arrived(back_full.at[t, parts, :], d_recv.at[t])
        outs.append(dot(l_full[t], back_full[t]).astype(BF16))
    half = chunk // 2
    for j in range(chips // per):
        both = jnp.concatenate([o[j * half : (j + 1) * half] for o in outs], axis=0)
        part = dot(sort_out[...], both).astype(BF16)
        out_own[j * half : (j + 1) * half] = part[:half]
        out_send[j * half : (j + 1) * half] = part[half:]
    share = remote(out_send, out_recv, y_send, y_recv, sibling)
    share.start()
    share.wait()
    near = out_own[...].astype(F32).reshape(chips, 2 * rows, LANES)
    away = out_recv[...].astype(F32).reshape(chips, 2 * rows, LANES)
    send_e[...] = jnp.concatenate([near, away], axis=1).astype(BF16)

    def step(i, carry):
        to = lax.rem(chip + i * 37, chips)
        remote(send_e.at[to], recv_e.at[chip], e_send, e_recv, (x, to * 2 + core)).start()
        return carry
    lax.fori_loop(1, chips, step, 0)
    recv_e[chip] = send_e[chip]
    for t in range(2):
        block = g_full[t]
        left_term = dot(g_full[t, column(x), :], block, 1, 1)
        new_left_ref[t] = jnp.where(used[t] > 0.0, 0.95 * stat_l[t] + 0.05 * left_term, stat_l[t])
        right_term = dot(g_full[t, :, column(x)], block, 0, 0)
        new_right_ref[t] = jnp.where(used[t] > 0.0, 0.95 * stat_r[t] + 0.05 * right_term, stat_r[t])
    arrived(recv_e.at[pl.ds(0, chips - 1)], e_recv)
    picked = dot(place[...], recv_e[...].reshape(chips * 4 * rows, LANES))
    update_ref[...] = picked.astype(BF16).reshape(layers, rows, blocks_per, LANES)

    arrived(raw.at[pl.ds(0, 3)], a_send)
    arrived(send_b.at[pl.ds(0, chips - 1)], b_send)
    arrived(send_e.at[pl.ds(0, chips - 1)], e_send)
    arrived(g_full.at[:, parts, :], c_send)
    arrived(r_full.at[:, parts, :], r_send)
    arrived(l_full.at[:, parts, :], l_send)
    arrived(back_full.at[:, parts, :], d_send)


def local(gradient, owner_slot, stat_left, stat_right, second_moment, basis_left, basis_right):
    layers, row_dev, columns = gradient.shape[1:]
    capacity, quarter, order = basis_right.shape
    blocks_per = columns // order
    chips = LINE * LINE
    many = layers * blocks_per * row_dev
    pieces = gradient.reshape(layers, row_dev, blocks_per, order)
    vmem = pl.BlockSpec(memory_space=pltpu.VMEM)
    anywhere = pl.BlockSpec(memory_space=pl.ANY)
    dma = pltpu.SemaphoreType.DMA
    message = (chips, 4 * row_dev, quarter)
    stat = (capacity, quarter, order)
    full = (capacity, order, order)
    return pl.pallas_call(
        kernel,
        name="soap_step",
        out_shape=(
            jax.ShapeDtypeStruct((layers, row_dev, blocks_per, quarter), BF16),
            jax.ShapeDtypeStruct(stat, F32),
            jax.ShapeDtypeStruct(stat, F32),
            jax.ShapeDtypeStruct(stat, F32),
        ),
        in_specs=[vmem, vmem] + [anywhere] * 5,
        out_specs=[vmem] * 4,
        scratch_shapes=[
            pltpu.VMEM((4, layers, row_dev, blocks_per, quarter), BF16),
            pltpu.VMEM((2, many, quarter), BF16),
            pltpu.VMEM((chips * 2 * row_dev, many), BF16),
            pltpu.VMEM((many, chips * 4 * row_dev), BF16),
            pltpu.VMEM((256, 256), BF16),
            pltpu.VMEM((256, 256), BF16),
            pltpu.VMEM(message, BF16),
            pltpu.VMEM(message, BF16),
            pltpu.VMEM(full, BF16),
            pltpu.VMEM(full, BF16),
            pltpu.VMEM(full, BF16),
            pltpu.VMEM((capacity, order, quarter), BF16),
            pltpu.VMEM((capacity, quarter, order), BF16),
            pltpu.VMEM((capacity, order, quarter), BF16),
            pltpu.VMEM((order, quarter), BF16),
            pltpu.VMEM((order, quarter), BF16),
            pltpu.VMEM((order, quarter), BF16),
            pltpu.VMEM(message, BF16),
            pltpu.VMEM(message, BF16),
            pltpu.VMEM(stat, F32),
            pltpu.VMEM(stat, F32),
            pltpu.VMEM(stat, F32),
            dma((9,)),
            dma, dma,
            dma, dma,
            dma, dma,
            dma, dma((2,)),
            dma, dma,
            dma, dma,
            dma, dma((2,)),
            dma, dma,
            dma, dma,
            pltpu.SemaphoreType.REGULAR,
        ],
        compiler_params=pltpu.CompilerParams(
            collective_id=0, has_side_effects=True, vmem_limit_bytes=40 << 20
        ),
    )(owner_slot, pieces, stat_left, stat_right, second_moment, basis_left, basis_right)


def solution(mesh):
    placed = (
        P("dp", None, "fsdp", None),
        P(),
        P("fsdp", "dp", None),
        P("fsdp", "dp", None),
        P("fsdp", "dp", None),
        P("fsdp", None, "dp"),
        P("fsdp", "dp", None),
    )
    return jax.shard_map(
        local,
        mesh=mesh,
        in_specs=placed,
        out_specs=(
            P(None, "fsdp", None, "dp"),
            P("fsdp", "dp", None),
            P("fsdp", "dp", None),
            P("fsdp", "dp", None),
        ),
        check_vma=False,
    )
```

time: 212 us -> 86.6 us (0.41)
  waiting for transfers between devices: 128 us -> 0 us
  Pallas kernels: 0 us -> 77.5 us
  starting transfers between devices: 34.3 us -> 0 us
  local copies, waits for them, and re-layouts: 27.6 us -> 8.17 us
  between operations: 13.9 us -> 0.69 us
  matrix products: 7.29 us -> 0 us
    pallas_call x0 -> x1, Pallas kernels: none -> 77.5 us  [local(): pl.pallas_call(kernel, name='soap_step', out_shape=(jax.ShapeDtypeStruct(...]
    psum x1 -> x0, waiting for transfers between devices: 55.6 us -> none  [local(): lax.psum(owned.astype(jnp.float32).astype(jnp.bfloat16), 'dp')]
    all_to_all x2 -> x0, waiting for transfers between devices: 42.9 us -> none  [the longest x1 30.1 us: local(): lax.all_to_all(filled, 'fsdp', split_axis=0, concat_axis=1, tiled=True)]
    all_to_all x2 -> x0, starting transfers between devices: 34.1 us -> none  [the longest x1 18.4 us: local(): lax.all_to_all(filled, 'fsdp', split_axis=0, concat_axis=1, tiled=True)]
    reduce_scatter x1 -> x0, waiting for transfers between devices: 28.4 us -> none  [local(): lax.psum_scatter(partial_value.astype(jnp.bfloat16), 'dp', scatter_dimens...]
    scatter x2 -> x0, local copies, waits for them, and re-layouts: 15.4 us -> none  [the longest x1 14.4 us: local(): jnp.zeros((slot_count,) + pieces.shape[1:], pieces.dtype).at[slot_flat]]
    dot_general x4 -> x0, matrix products: 7.29 us -> none  [the longest x1 3.09 us: local(): jnp.einsum('sqj,sjk->sqk', half_turn, right_full, preferred_element_type=...]
    unnamed x15 -> x16, local copies, waits for them, and re-layouts: 1.88 us -> 6.67 us
  transfers between devices with their start and end apart: 5 -> 0, of which waited for: 4 -> 0; matrix products, arithmetic and copies ran while one was open for 3% -> 0% of each run, Pallas kernels for 0% -> 0%
where the time goes in v1:
time: 86.6 us; the launch traced here: 86.3 us
  Pallas kernels  77.5 us (89%)
  local copies, waits for them, and re-layouts  8.17 us (9%)
    pallas_call x1, Pallas kernels, local(): pl.pallas_call(kernel, name='soap_step', out_shape=(jax.ShapeDtypeStruct(...  77.5 us
    unnamed x16, local copies, waits for them, and re-layouts  6.67 us

profile of v1, /device:TPU:1, one launch (start us, length us, event | category | flops | bytes accessed | tf_op | source)
XLA Modules:
  0.0 86.3 jit_solution(15718645137384632677)
XLA Ops:
  0.6 0.0 copy-start.1
  0.6 0.0 copy-start
  0.7 1.5 %reshape.11.grad_ref = bf16[8,4,16,512]{3,2,1,0:T(8,128)(2,1)S(1)} reshape(bf16[1,8,4,8192]{3,2,1,0:T(4,128)(2,1)} %param.7) | data formatting | bytes 1048576 | tf_op jit(solution)/shard_map/reshape | solution.py:246
  2.2 0.0 copy-done.1
  2.2 0.0 copy-done
  2.2 0.0 copy-start.2
  2.2 1.0 %copy-done.2 = f32[2,128,512]{2,1,0:T(8,128)S(1)} copy-done((f32[2,128,512]{2,1,0:T(8,128)S(1)}, f32[2,128,512]{2,1,0:T(8,128)}, u32[]{:S(2)}) %copy-start.2) | copy-done | bytes 524312
  3.2 0.0 copy-start.3
  3.2 0.9 %copy-done.3 = bf16[2,512,128]{2,1,0:T(8,128)(2,1)S(1)} copy-done((bf16[2,512,128]{2,1,0:T(8,128)(2,1)S(1)}, bf16[2,512,128]{2,1,0:T(8,128)(2,1)}, u32[]{:S(2)}) %copy-start.3) | copy-done | bytes 262168
  4.2 0.0 copy-start.4
  4.2 0.9 %copy-done.4 = bf16[2,128,512]{2,1,0:T(8,128)(2,1)S(1)} copy-done((bf16[2,128,512]{2,1,0:T(8,128)(2,1)S(1)}, bf16[2,128,512]{2,1,0:T(8,128)(2,1)}, u32[]{:S(2)}) %copy-start.4) | copy-done | bytes 262168
  5.1 0.0 copy-start.5
  5.1 0.7 copy-done.5
  5.8 77.5 %soap_step.1 = (bf16[8,4,16,128]{3,2,1,0:T(8,128)(2,1)S(1)}, f32[2,128,512]{2,1,0:T(8,128)S(1)}, f32[2,128,512]{2,1,0:T(8,128)S(1)}, f32[2,128,512]{2,1,0:T(8,128)S(1)}) custom-call(s32[8,16]{1,0:T(8,128)S(1)} %copy-done.5, bf16[8,4,16,512]{3,2,1,0:T(8,128)(2,1)S(1)} %reshape.11.grad_ref, f32[2,128,512]{2,1,0:T(8,128)S(1)} %copy-done, ...), custom_call_target="tpu_custom_call" | custom-call | tf_op jit(solution)/shard_map/soap_step/pallas_call | solution.py:253
  83.3 0.7 copy.15
  83.9 0.8 copy.16
  84.7 0.8 copy.17
  85.5 0.8 copy.18
Async XLA Ops:
  0.6 1.5 %copy-start.1 = (f32[2,128,512]{2,1,0:T(8,128)S(1)}, f32[2,128,512]{2,1,0:T(8,128)}, u32[]{:S(2)}) copy-start(f32[2,128,512]{2,1,0:T(8,128)} %right_ref.1) | copy-start | bytes 1572868
  0.6 1.5 %copy-start = (f32[2,128,512]{2,1,0:T(8,128)S(1)}, f32[2,128,512]{2,1,0:T(8,128)}, u32[]{:S(2)}) copy-start(f32[2,128,512]{2,1,0:T(8,128)} %left_ref.1) | copy-start | bytes 1572868
  2.2 1.0 %copy-start.2 = (f32[2,128,512]{2,1,0:T(8,128)S(1)}, f32[2,128,512]{2,1,0:T(8,128)}, u32[]{:S(2)}) copy-start(f32[2,128,512]{2,1,0:T(8,128)} %moment_ref.1) | copy-start | bytes 1572868
  3.2 0.9 %copy-start.3 = (bf16[2,512,128]{2,1,0:T(8,128)(2,1)S(1)}, bf16[2,512,128]{2,1,0:T(8,128)(2,1)}, u32[]{:S(2)}) copy-start(bf16[2,512,128]{2,1,0:T(8,128)(2,1)} %bl_ref.1) | copy-start | bytes 786436
  4.2 0.9 %copy-start.4 = (bf16[2,128,512]{2,1,0:T(8,128)(2,1)S(1)}, bf16[2,128,512]{2,1,0:T(8,128)(2,1)}, u32[]{:S(2)}) copy-start(bf16[2,128,512]{2,1,0:T(8,128)(2,1)} %br_ref.1) | copy-start | bytes 786436
  5.1 0.7 copy-start.5

commit v2 on v1

v2 whole, which is shorter than its diff:
```python
import functools

import jax
import jax.numpy as jnp
from jax import lax
from jax.experimental import pallas as pl
from jax.experimental.pallas import tpu as pltpu
from jax.sharding import PartitionSpec as P

epsilon = 1e-08
MESH = pl.DeviceIdType.MESH
F32, BF16, I32 = jnp.float32, jnp.bfloat16, jnp.int32
LINE = 8
LANES = 128


def iota(shape, dim):
    return lax.broadcasted_iota(I32, shape, dim)


def dot(a, b, ca=1, cb=0):
    return lax.dot_general(a, b, (((ca,), (cb,)), ((), ())), preferred_element_type=F32)


def one_hot(rows, columns):
    return jnp.where(rows == columns, 1.0, 0.0).astype(BF16)


def kernel(
    slot_ref, grad_ref, left_ref, right_ref, moment_ref, bl_ref, br_ref,
    update_ref, new_left_ref, new_right_ref, new_moment_ref,
    slot_vmem, raw, mean, pick, place, sort_in, sort_own, sort_sib,
    send_b, recv_b, g_full, l_full, r_full, l_own, back_own, back_full,
    out_own, out_sib, send_e, recv_e, stat_l, stat_r, stat_m, update,
    local_sem, store_sem, a_send, a_recv, x_send, x_recv, b_send, b_recv, c_send, c_recv,
    l_send, l_near, l_far, l_last, r_send, r_near, r_far, d_send, d_recv, y_send, y_recv,
    e_send, e_recv, tokens,
):
    x = lax.axis_index("dp")
    f = lax.axis_index("fsdp")
    groups = 4
    core = lax.rem(f, 2)
    chip = f // 2
    z, y = chip // LINE, lax.rem(chip, LINE)
    chips = LINE * LINE
    sibling = (x, f + 1 - 2 * core)
    layers, rows, blocks_per, _ = grad_ref.shape
    many = layers * rows * blocks_per
    order = g_full.shape[1]
    quarter = order // groups
    half = quarter // 2
    parts = pl.ds(0, order - quarter)

    def x_peer(d):
        return lax.rem(x + d + groups, groups)

    def device(zz, yy):
        return (x, (zz * LINE + yy) * 2 + core)

    def z_peer(d):
        return device(lax.rem(z + d + LINE, LINE), y)

    def y_peer(d):
        return device(z, lax.rem(y + d + LINE, LINE))

    def column(p):
        return pl.ds(pl.multiple_of(p * LANES, LANES), LANES)

    def row_half(p, size, which):
        return pl.ds(pl.multiple_of(p * size + which * (size // 2), size // 2), size // 2)

    def remote(src, dst, send, recv, to):
        return pltpu.make_async_remote_copy(
            src_ref=src, dst_ref=dst, send_sem=send, recv_sem=recv,
            device_id=to, device_id_type=MESH,
        )

    def signal(sem, to):
        pl.semaphore_signal(sem, inc=1, device_id=to, device_id_type=MESH)

    pending = {}

    def started(name, ref, sem):
        pending[name] = lambda: pltpu.make_async_copy(ref, ref, sem).wait()

    def arrived(name):
        pending.pop(name)()

    def finish():
        for name in list(pending):
            arrived(name)

    barrier = pltpu.get_barrier_semaphore()
    for d in (2, 1, -1):
        signal(barrier, (x_peer(d), f))
    for d in (1, -1):
        signal(barrier, z_peer(d))
        signal(barrier, y_peer(d))
    signal(barrier, sibling)

    loads = [
        pltpu.make_async_copy(slot_ref, slot_vmem, local_sem.at[0]),
        pltpu.make_async_copy(grad_ref.at[:, :, :, column(x)], raw.at[3], local_sem.at[1]),
        pltpu.make_async_copy(bl_ref, l_own, local_sem.at[2]),
        pltpu.make_async_copy(left_ref, stat_l, local_sem.at[3]),
        pltpu.make_async_copy(right_ref, stat_r, local_sem.at[4]),
        pltpu.make_async_copy(moment_ref, stat_m, local_sem.at[5]),
    ]
    for t in range(2):
        loads.append(pltpu.make_async_copy(bl_ref.at[t], l_full.at[t, :, column(x)], local_sem.at[6 + t]))
        loads.append(pltpu.make_async_copy(br_ref.at[t], r_full.at[t, column(x), :], local_sem.at[8 + t]))
    for i, load in enumerate(loads):
        load.start()
        pending["load", i] = load.wait
    pl.semaphore_wait(barrier, 8)

    for d in (2, 1, -1):
        p = x_peer(d)
        at = {2: 1, 1: 0, -1: 2}[d]
        remote(grad_ref.at[:, :, :, column(p)], raw.at[at], a_send, a_recv, (p, f)).start()
    started("groups", raw.at[pl.ds(0, 3)], a_recv)
    started("groups sent", raw.at[pl.ds(0, 3)], a_send)

    def greet(i, peers):
        for d in (1, -1):
            signal(tokens.at[i], peers(d * (2 if i in (1, 4) else 1)))
        pending["token", i] = lambda: pl.semaphore_wait(tokens.at[i], 2)

    greet(0, z_peer)

    arrived(("load", 0))
    slots = slot_vmem[...].astype(F32).astype(BF16)
    spread = one_hot(lax.rem(iota((blocks_per, many), 1), blocks_per), iota((blocks_per, many), 0))
    wide = dot(slots, spread)
    own_layer = iota((layers, many), 1) // (rows * blocks_per) == iota((layers, many), 0)
    slot_lane = jnp.sum(jnp.where(own_layer, wide, 0.0), axis=0, keepdims=True).astype(I32)
    row_lane = lax.rem(iota((1, many), 1) // blocks_per, rows)
    owner_lane = slot_lane // 2
    code_lane = jnp.where(
        lax.rem(owner_lane, 2) == core,
        (owner_lane // 2) * 2 * rows + lax.rem(slot_lane, 2) * rows + row_lane, -1,
    )
    used = [jnp.max(jnp.where(slot_lane == 2 * f + t, 1.0, 0.0), axis=1, keepdims=True) for t in range(2)]
    pick[...] = one_hot(code_lane, iota((chips * 2 * rows, many), 0))
    arrived(("token", 0))
    greet(1, z_peer)
    tall_spread = one_hot(lax.rem(iota((many, blocks_per), 0), blocks_per), iota((many, blocks_per), 1))
    tall = dot(tall_spread, slots, 1, 1)
    tall_layer = iota((many, layers), 0) // (rows * blocks_per) == iota((many, layers), 1)
    slot_col = jnp.sum(jnp.where(tall_layer, tall, 0.0), axis=1, keepdims=True).astype(I32)
    row_col = lax.rem(iota((many, 1), 0) // blocks_per, rows)
    owner_col = slot_col // 2
    far = jnp.where(lax.rem(owner_col, 2) == core, 0, 1)
    code_col = ((owner_col // 2) * 2 + far) * 2 * rows + lax.rem(slot_col, 2) * rows + row_col
    place[...] = one_hot(code_col, iota((many, chips * 4 * rows), 1))
    arrived(("token", 1))
    greet(2, y_peer)
    chunk = 256
    part = chunk // 2
    per = chunk // (4 * rows)
    ro, co = iota((chunk, 1), 0), iota((1, chunk), 1)
    far_o = lax.rem(lax.rem(ro // rows, 2) + core, 2)
    want = ((lax.rem(ro // (2 * rows), per) * 2 + far_o) * 2 + ro // part) * rows + lax.rem(ro, rows)
    sort_in[...] = one_hot(want, co)
    chip_o = ro // (4 * rows)
    t_o = lax.rem(ro // rows, 2)
    want = ((t_o * per + chip_o) * 2 + core) * rows + lax.rem(ro, rows)
    far_o = lax.rem(ro // (2 * rows), 2)
    sort_own[...] = one_hot(jnp.where(far_o == 0, want, -1), co)
    sort_sib[...] = one_hot(jnp.where(far_o == 1, want, -1), co)
    arrived(("token", 2))
    greet(3, y_peer)
    for i in range(1, len(loads)):
        arrived(("load", i))
    arrived(("token", 3))
    greet(4, y_peer)

    arrived("groups")
    total = raw[0].astype(F32) + raw[1].astype(F32) + raw[2].astype(F32) + raw[3].astype(F32)
    mean[0] = (total * (1.0 / groups)).astype(BF16).reshape(many, LANES)
    share = remote(mean.at[0], mean.at[1], x_send, x_recv, sibling)
    share.start()
    pending["mean"] = share.wait
    for t in range(2):
        for d in (1, -1):
            mine = r_full.at[t, column(x), :]
            remote(mine, mine, r_send, r_near, (x_peer(d), f)).start()
    for d in (1, -1):
        mine = l_full.at[0, :, column(x)]
        remote(mine, mine, l_send, l_near, (x_peer(d), f)).start()
    started("right near", r_full.at[:, pl.ds(0, 2 * quarter), :], r_near)
    started("right sent", r_full.at[:, pl.ds(0, 2 * quarter), :], r_send)
    started("left near", l_full.at[0, pl.ds(0, 2 * quarter), :], l_near)
    started("left sent", l_full.at[0, pl.ds(0, 2 * quarter), :], l_send)

    near = dot(pick[...], mean[0]).reshape(chips, 2 * rows, LANES)
    arrived("mean")
    away = dot(pick[...], mean[1]).reshape(chips, 2 * rows, LANES)
    send_b[...] = jnp.concatenate([near, away], axis=1).astype(BF16)

    arrived(("token", 4))

    def all_to_all(name, src, dst, send, recv):
        def step(i, carry):
            to = lax.rem(chip + i * 37, chips)
            remote(src.at[to], dst.at[chip], send, recv, (x, to * 2 + core)).start()
            return carry
        lax.fori_loop(1, chips, step, 0)
        dst[chip] = src[chip]
        started(name, dst.at[pl.ds(0, chips - 1)], recv)
        started(name + " sent", src.at[pl.ds(0, chips - 1)], send)

    all_to_all("rows", send_b, recv_b, b_send, b_recv)

    arrived("right near")
    for t in range(2):
        for i, d in enumerate((1, -1)):
            piece = r_full.at[t, row_half(x_peer(-d), quarter, i), :]
            remote(piece, piece, r_send, r_far, (x_peer(d), f)).start()
    started("right", r_full.at[:, pl.ds(0, quarter), :], r_far)
    started("right sent", r_full.at[:, parts, :], r_send)

    arrived("rows")
    for j in range(chips // per):
        rows_j = dot(sort_in[...], recv_b[j * per : (j + 1) * per].reshape(chunk, LANES)).astype(BF16)
        for t in range(2):
            g_full[t, j * part : (j + 1) * part, column(x)] = rows_j[t * part : (t + 1) * part]
    for t in range(2):
        for d in (2, 1, -1):
            mine = g_full.at[t, :, column(x)]
            remote(mine, mine, c_send, c_recv.at[t], (x_peer(d), f)).start()
        started(("block", t), g_full.at[t, parts, :], c_recv.at[t])
    started("blocks sent", g_full.at[:, parts, :], c_send)
    arrived("left near")
    for i, d in enumerate((1, -1)):
        piece = l_full.at[0, pl.ds(i * (order // 2), order // 2), column(x_peer(-d))]
        remote(piece, piece, l_send, l_far, (x_peer(d), f)).start()
    started("left 0", l_full.at[0, pl.ds(0, quarter), :], l_far)
    started("left sent", l_full.at[0, parts, :], l_send)
    arrived("right")

    def block_step(t):
        block = g_full[t]
        right = r_full[t]
        half_turn = dot(l_own[t], block, 0, 0).astype(BF16)
        rotated = dot(half_turn, right)
        moment = 0.95 * stat_m[t] + 0.05 * rotated * rotated
        stat_m[t] = jnp.where(used[t] > 0.0, moment, stat_m[t])
        scaled = (rotated / (jnp.sqrt(moment) + epsilon)).astype(BF16)
        back_own[t] = dot(scaled, right, 1, 1).astype(BF16)
        for d in (2, 1, -1):
            p = x_peer(d)
            remote(
                back_own.at[t, :, column(p)], back_full.at[t, column(x), :],
                d_send, d_recv.at[t], (p, f),
            ).start()
        started(("back", t), back_full.at[t, parts, :], d_recv.at[t])
        started("back sent", back_full.at[pl.ds(0, t + 1), parts, :], d_send)
        back_full[t, column(x), :] = back_own[t, :, column(x)]

    def out_step(t):
        arrived(("back", t))
        out_own[t] = dot(l_full[t], back_full[t]).astype(BF16)
        remote(out_own.at[t], out_sib.at[t], y_send, y_recv.at[t], sibling).start()
        started(("out", t), out_sib.at[t], y_recv.at[t])
        started("out sent", out_own.at[pl.ds(0, t + 1)], y_send)

    arrived(("block", 0))
    block_step(0)
    arrived(("block", 1))
    for d in (2, 1, -1):
        mine = l_full.at[1, :, column(x)]
        remote(mine, mine, l_send, l_last, (x_peer(d), f)).start()
    started("left 1", l_full.at[1, parts, :], l_last)
    started("left sent", l_full.at[:, parts, :], l_send)
    block_step(1)
    arrived("left 0")
    out_step(0)
    arrived("left 1")
    out_step(1)
    def sort_rows(ref, sort, j):
        both = jnp.concatenate([ref[t, j * part : (j + 1) * part] for t in range(2)], axis=0)
        return dot(sort[...], both)

    mine = [sort_rows(out_own, sort_own, j) for j in range(chips // per)]
    arrived(("out", 0))
    arrived(("out", 1))
    for j in range(chips // per):
        both = (mine[j] + sort_rows(out_sib, sort_sib, j)).astype(BF16)
        send_e[j * per : (j + 1) * per] = both.reshape(per, 4 * rows, LANES)

    all_to_all("update", send_e, recv_e, e_send, e_recv)
    stores = []

    def store(src, dst):
        copy = pltpu.make_async_copy(src, dst, store_sem.at[len(stores)])
        copy.start()
        pending["store", len(stores)] = copy.wait
        stores.append(copy)

    store(stat_m, new_moment_ref)
    for t in range(2):
        block = g_full[t]
        left_term = dot(g_full[t, column(x), :], block, 1, 1)
        stat_l[t] = jnp.where(used[t] > 0.0, 0.95 * stat_l[t] + 0.05 * left_term, stat_l[t])
        store(stat_l.at[t], new_left_ref.at[t])
        right_term = dot(g_full[t, :, column(x)], block, 0, 0)
        stat_r[t] = jnp.where(used[t] > 0.0, 0.95 * stat_r[t] + 0.05 * right_term, stat_r[t])
        store(stat_r.at[t], new_right_ref.at[t])
    arrived("update")
    picked = dot(place[...], recv_e[...].reshape(chips * 4 * rows, LANES))
    update[...] = picked.astype(BF16).reshape(layers, rows, blocks_per, LANES)
    store(update, update_ref)
    finish()


def store_kernel(*refs):
    count = len(refs) // 3
    semaphores = refs[-1]
    moves = [
        (
            pltpu.make_async_copy(refs[i], refs[2 * count + i], semaphores.at[i]),
            pltpu.make_async_copy(refs[2 * count + i], refs[count + i], semaphores.at[count + i]),
        )
        for i in range(count)
    ]
    for load, _ in moves:
        load.start()
    for load, store in moves:
        load.wait()
        store.start()
    for _, store in moves:
        store.wait()


def local(gradient, owner_slot, stat_left, stat_right, second_moment, basis_left, basis_right):
    layers, row_dev, columns = gradient.shape[1:]
    capacity, quarter, order = basis_right.shape
    blocks_per = columns // order
    chips = LINE * LINE
    many = layers * blocks_per * row_dev
    pieces = gradient.reshape(layers, row_dev, blocks_per, order)
    hbm = pl.BlockSpec(memory_space=pltpu.HBM)
    dma = pltpu.SemaphoreType.DMA
    message = (chips, 4 * row_dev, quarter)
    stat = (capacity, quarter, order)
    full = (capacity, order, order)
    results = pl.pallas_call(
        kernel,
        name="soap_step",
        out_shape=(
            jax.ShapeDtypeStruct((layers, row_dev, blocks_per, quarter), BF16),
            jax.ShapeDtypeStruct(stat, F32),
            jax.ShapeDtypeStruct(stat, F32),
            jax.ShapeDtypeStruct(stat, F32),
        ),
        in_specs=[hbm] * 7,
        out_specs=[hbm] * 4,
        scratch_shapes=[
            pltpu.VMEM(owner_slot.shape, I32),
            pltpu.VMEM((4, layers, row_dev, blocks_per, quarter), BF16),
            pltpu.VMEM((2, many, quarter), BF16),
            pltpu.VMEM((chips * 2 * row_dev, many), BF16),
            pltpu.VMEM((many, chips * 4 * row_dev), BF16),
            pltpu.VMEM((256, 256), BF16),
            pltpu.VMEM((256, 256), BF16),
            pltpu.VMEM((256, 256), BF16),
            pltpu.VMEM(message, BF16),
            pltpu.VMEM(message, BF16),
            pltpu.VMEM(full, BF16),
            pltpu.VMEM(full, BF16),
            pltpu.VMEM(full, BF16),
            pltpu.VMEM((capacity, order, quarter), BF16),
            pltpu.VMEM((capacity, quarter, order), BF16),
            pltpu.VMEM((capacity, order, quarter), BF16),
            pltpu.VMEM((capacity, order, quarter), BF16),
            pltpu.VMEM((capacity, order, quarter), BF16),
            pltpu.VMEM(message, BF16),
            pltpu.VMEM(message, BF16),
            pltpu.VMEM(stat, F32),
            pltpu.VMEM(stat, F32),
            pltpu.VMEM(stat, F32),
            pltpu.VMEM((layers, row_dev, blocks_per, quarter), BF16),
            dma((10,)),
            dma((6,)),
            dma, dma,
            dma, dma,
            dma, dma,
            dma, dma((2,)),
            dma, dma, dma, dma,
            dma, dma, dma,
            dma, dma((2,)),
            dma, dma((2,)),
            dma, dma,
            pltpu.SemaphoreType.REGULAR((5,)),
        ],
        compiler_params=pltpu.CompilerParams(
            collective_id=0, has_side_effects=True, vmem_limit_bytes=60 << 20
        ),
    )(owner_slot, pieces, stat_left, stat_right, second_moment, basis_left, basis_right)
    return pl.pallas_call(
        store_kernel,
        name="store",
        out_shape=tuple(jax.ShapeDtypeStruct(r.shape, r.dtype) for r in results),
        in_specs=[hbm] * 4,
        out_specs=[hbm] * 4,
        scratch_shapes=[pltpu.VMEM(r.shape, r.dtype) for r in results] + [dma((8,))],
        compiler_params=pltpu.CompilerParams(vmem_limit_bytes=60 << 20),
    )(*results)


def solution(mesh):
    placed = (
        P("dp", None, "fsdp", None),
        P(),
        P("fsdp", "dp", None),
        P("fsdp", "dp", None),
        P("fsdp", "dp", None),
        P("fsdp", None, "dp"),
        P("fsdp", "dp", None),
    )
    return jax.shard_map(
        local,
        mesh=mesh,
        in_specs=placed,
        out_specs=(
            P(None, "fsdp", None, "dp"),
            P("fsdp", "dp", None),
            P("fsdp", "dp", None),
            P("fsdp", "dp", None),
        ),
        check_vma=False,
    )
```

time: 86.6 us -> 76.8 us (0.89)
  local copies, waits for them, and re-layouts: 8.17 us -> 2.21 us
  Pallas kernels: 77.5 us -> 73.8 us
    unnamed x16 -> x0, local copies, waits for them, and re-layouts: 6.67 us -> none
    pallas_call x1, Pallas kernels: 77.5 us -> 71.5 us  [local(): pl.pallas_call(kernel, name='soap_step', out_shape=(jax.ShapeDtypeStruct(...]
    pallas_call x0 -> x1, Pallas kernels: none -> 2.32 us  [local(): pl.pallas_call(store_kernel, name='store', out_shape=tuple((jax.ShapeDtyp...]
where the time goes in v2:
time: 76.8 us; the launch traced here: 76.6 us
  Pallas kernels  73.8 us (96%)
  local copies, waits for them, and re-layouts  2.21 us (3%)
    pallas_call x1, Pallas kernels, local(): pl.pallas_call(kernel, name='soap_step', out_shape=(jax.ShapeDtypeStruct(...  71.5 us
    pallas_call x1, Pallas kernels, local(): pl.pallas_call(store_kernel, name='store', out_shape=tuple((jax.ShapeDtyp...  2.32 us
    reshape x1, local copies, waits for them, and re-layouts, local(): pieces = gradient.reshape(layers, row_dev, blocks_per, order)  2.21 us

profile of v2, /device:TPU:1, one launch (start us, length us, event | category | flops | bytes accessed | tf_op | source)
XLA Modules:
  0.0 76.6 jit_solution(12085876201819563077)
XLA Ops:
  0.6 2.2 %reshape.11.grad_ref = bf16[8,4,16,512]{3,2,1,0:T(8,128)(2,1)} reshape(bf16[1,8,4,8192]{3,2,1,0:T(4,128)(2,1)} %param.7) | data formatting | bytes 1048576 | tf_op jit(solution)/shard_map/reshape | solution.py:342
  2.8 71.5 %soap_step.1 = (bf16[8,4,16,128]{3,2,1,0:T(8,128)(2,1)}, f32[2,128,512]{2,1,0:T(8,128)}, f32[2,128,512]{2,1,0:T(8,128)}, f32[2,128,512]{2,1,0:T(8,128)}) custom-call(s32[8,16]{1,0:T(8,128)} %slot_ref.1, bf16[8,4,16,512]{3,2,1,0:T(8,128)(2,1)} %reshape.11.grad_ref, f32[2,128,512]{2,1,0:T(8,128)} %left_ref.1, f32[2,128,512]{2,1,0:T(8,128)} %right_ref.1, ...), custom_call_target="tpu_custom_call" | custom-call | tf_op jit(solution)/shard_map/soap_step/pallas_call | solution.py:348
  74.3 2.3 %store.1 = (bf16[8,4,16,128]{3,2,1,0:T(8,128)(2,1)}, f32[2,128,512]{2,1,0:T(8,128)}, f32[2,128,512]{2,1,0:T(8,128)}, f32[2,128,512]{2,1,0:T(8,128)}) custom-call(bf16[8,4,16,128]{3,2,1,0:T(8,128)(2,1)} %get-tuple-element.8.refs_0_, f32[2,128,512]{2,1,0:T(8,128)} %get-tuple-element.9.refs_1_, f32[2,128,512]{2,1,0:T(8,128)} %get-tuple-element.10.refs_2_, ...), custom_call_target="tpu_custom_call" | custom-call | tf_op jit(solution)/shard_map/store/pallas_call | solution.py:401

commit v3 on v2

--- a/solution.py
+++ b/solution.py
@@ -14,6 +14,16 @@
 LANES = 128
 
 
+def hops(d):
+    return min(d, LINE - d)
+
+
+far_first = sorted(
+    ((dz, dy) for dz in range(LINE) for dy in range(LINE) if dz or dy),
+    key=lambda step: -hops(step[0]) - hops(step[1]),
+)
+
+
 def iota(shape, dim):
     return lax.broadcasted_iota(I32, shape, dim)
 
@@ -31,8 +41,8 @@
     update_ref, new_left_ref, new_right_ref, new_moment_ref,
     slot_vmem, raw, mean, pick, place, sort_in, sort_own, sort_sib,
     send_b, recv_b, g_full, l_full, r_full, l_own, back_own, back_full,
-    out_own, out_sib, send_e, recv_e, stat_l, stat_r, stat_m, update,
-    local_sem, store_sem, a_send, a_recv, x_send, x_recv, b_send, b_recv, c_send, c_recv,
+    out_own, out_sib, send_e, recv_e, stat_l, stat_r, stat_m,
+    local_sem, a_send, a_recv, x_send, x_recv, b_send, b_recv, c_send, c_near, c_far,
     l_send, l_near, l_far, l_last, r_send, r_near, r_far, d_send, d_recv, y_send, y_recv,
     e_send, e_recv, tokens,
 ):
@@ -200,12 +210,13 @@
 
     arrived(("token", 4))
 
+    along_z = [lax.rem(z + d, LINE) for d in range(LINE)]
+    along_y = [lax.rem(y + d, LINE) for d in range(LINE)]
+
     def all_to_all(name, src, dst, send, recv):
-        def step(i, carry):
-            to = lax.rem(chip + i * 37, chips)
+        for dz, dy in far_first:
+            to = along_z[dz] * LINE + along_y[dy]
             remote(src.at[to], dst.at[chip], send, recv, (x, to * 2 + core)).start()
-            return carry
-        lax.fori_loop(1, chips, step, 0)
         dst[chip] = src[chip]
         started(name, dst.at[pl.ds(0, chips - 1)], recv)
         started(name + " sent", src.at[pl.ds(0, chips - 1)], send)
@@ -220,23 +231,36 @@
     started("right", r_full.at[:, pl.ds(0, quarter), :], r_far)
     started("right sent", r_full.at[:, parts, :], r_send)
 
-    arrived("rows")
-    for j in range(chips // per):
-        rows_j = dot(sort_in[...], recv_b[j * per : (j + 1) * per].reshape(chunk, LANES)).astype(BF16)
-        for t in range(2):
-            g_full[t, j * part : (j + 1) * part, column(x)] = rows_j[t * part : (t + 1) * part]
-    for t in range(2):
-        for d in (2, 1, -1):
-            mine = g_full.at[t, :, column(x)]
-            remote(mine, mine, c_send, c_recv.at[t], (x_peer(d), f)).start()
-        started(("block", t), g_full.at[t, parts, :], c_recv.at[t])
-    started("blocks sent", g_full.at[:, parts, :], c_send)
     arrived("left near")
     for i, d in enumerate((1, -1)):
         piece = l_full.at[0, pl.ds(i * (order // 2), order // 2), column(x_peer(-d))]
         remote(piece, piece, l_send, l_far, (x_peer(d), f)).start()
     started("left 0", l_full.at[0, pl.ds(0, quarter), :], l_far)
     started("left sent", l_full.at[0, parts, :], l_send)
+
+    arrived("rows")
+    for j in range(chips // per):
+        rows_j = dot(sort_in[...], recv_b[j * per : (j + 1) * per].reshape(chunk, LANES)).astype(BF16)
+        for t in range(2):
+            g_full[t, j * part : (j + 1) * part, column(x)] = rows_j[t * part : (t + 1) * part]
+    for t in range(2):
+        for d in (1, -1):
+            mine = g_full.at[t, :, column(x)]
+            remote(mine, mine, c_send, c_near.at[t], (x_peer(d), f)).start()
+        started(("block near", t), g_full.at[t, pl.ds(0, 2 * quarter), :], c_near.at[t])
+    started("blocks sent", g_full.at[:, pl.ds(0, 2 * quarter), :], c_send)
+    for t in range(2):
+        arrived(("block near", t))
+        for i, d in enumerate((1, -1)):
+            piece = g_full.at[t, pl.ds(i * (order // 2), order // 2), column(x_peer(-d))]
+            remote(piece, piece, c_send, c_far.at[t], (x_peer(d), f)).start()
+        started(("block", t), g_full.at[t, pl.ds(0, quarter), :], c_far.at[t])
+    started("blocks sent", g_full.at[:, parts, :], c_send)
+    for d in (2, 1, -1):
+        mine = l_full.at[1, :, column(x)]
+        remote(mine, mine, l_send, l_last, (x_peer(d), f)).start()
+    started("left 1", l_full.at[1, parts, :], l_last)
+    started("left sent", l_full.at[:, parts, :], l_send)
     arrived("right")
 
     def block_step(t):
@@ -245,7 +269,7 @@
         half_turn = dot(l_own[t], block, 0, 0).astype(BF16)
         rotated = dot(half_turn, right)
         moment = 0.95 * stat_m[t] + 0.05 * rotated * rotated
-        stat_m[t] = jnp.where(used[t] > 0.0, moment, stat_m[t])
+        new_moment_ref[t] = jnp.where(used[t] > 0.0, moment, stat_m[t])
         scaled = (rotated / (jnp.sqrt(moment) + epsilon)).astype(BF16)
         back_own[t] = dot(scaled, right, 1, 1).astype(BF16)
         for d in (2, 1, -1):
@@ -268,11 +292,6 @@
     arrived(("block", 0))
     block_step(0)
     arrived(("block", 1))
-    for d in (2, 1, -1):
-        mine = l_full.at[1, :, column(x)]
-        remote(mine, mine, l_send, l_last, (x_peer(d), f)).start()
-    started("left 1", l_full.at[1, parts, :], l_last)
-    started("left sent", l_full.at[:, parts, :], l_send)
     block_step(1)
     arrived("left 0")
     out_step(0)
@@ -290,47 +309,31 @@
         send_e[j * per : (j + 1) * per] = both.reshape(per, 4 * rows, LANES)
 
     all_to_all("update", send_e, recv_e, e_send, e_recv)
-    stores = []
-
-    def store(src, dst):
-        copy = pltpu.make_async_copy(src, dst, store_sem.at[len(stores)])
-        copy.start()
-        pending["store", len(stores)] = copy.wait
-        stores.append(copy)
-
-    store(stat_m, new_moment_ref)
     for t in range(2):
         block = g_full[t]
         left_term = dot(g_full[t, column(x), :], block, 1, 1)
-        stat_l[t] = jnp.where(used[t] > 0.0, 0.95 * stat_l[t] + 0.05 * left_term, stat_l[t])
-        store(stat_l.at[t], new_left_ref.at[t])
+        new_left_ref[t] = jnp.where(used[t] > 0.0, 0.95 * stat_l[t] + 0.05 * left_term, stat_l[t])
         right_term = dot(g_full[t, :, column(x)], block, 0, 0)
-        stat_r[t] = jnp.where(used[t] > 0.0, 0.95 * stat_r[t] + 0.05 * right_term, stat_r[t])
-        store(stat_r.at[t], new_right_ref.at[t])
+        new_right_ref[t] = jnp.where(used[t] > 0.0, 0.95 * stat_r[t] + 0.05 * right_term, stat_r[t])
     arrived("update")
     picked = dot(place[...], recv_e[...].reshape(chips * 4 * rows, LANES))
-    update[...] = picked.astype(BF16).reshape(layers, rows, blocks_per, LANES)
-    store(update, update_ref)
+    update_ref[...] = picked.astype(BF16).reshape(layers, rows, blocks_per, LANES)
     finish()
 
 
+def stay(array):
+    return pltpu.with_memory_space_constraint(array, pltpu.HBM)
+
+
 def store_kernel(*refs):
-    count = len(refs) // 3
-    semaphores = refs[-1]
-    moves = [
-        (
-            pltpu.make_async_copy(refs[i], refs[2 * count + i], semaphores.at[i]),
-            pltpu.make_async_copy(refs[2 * count + i], refs[count + i], semaphores.at[count + i]),
-        )
-        for i in range(count)
+    count = (len(refs) - 1) // 2
+    copies = [
+        pltpu.make_async_copy(refs[i], refs[count + i], refs[-1].at[i]) for i in range(count)
     ]
-    for load, _ in moves:
-        load.start()
-    for load, store in moves:
-        load.wait()
-        store.start()
-    for _, store in moves:
-        store.wait()
+    for copy in copies:
+        copy.start()
+    for copy in copies:
+        copy.wait()
 
 
 def local(gradient, owner_slot, stat_left, stat_right, second_moment, basis_left, basis_right):
@@ -340,6 +343,7 @@
     chips = LINE * LINE
     many = layers * blocks_per * row_dev
     pieces = gradient.reshape(layers, row_dev, blocks_per, order)
+    vmem = pl.BlockSpec(memory_space=pltpu.VMEM)
     hbm = pl.BlockSpec(memory_space=pltpu.HBM)
     dma = pltpu.SemaphoreType.DMA
     message = (chips, 4 * row_dev, quarter)
@@ -349,13 +353,13 @@
         kernel,
         name="soap_step",
         out_shape=(
-            jax.ShapeDtypeStruct((layers, row_dev, blocks_per, quarter), BF16),
-            jax.ShapeDtypeStruct(stat, F32),
-            jax.ShapeDtypeStruct(stat, F32),
-            jax.ShapeDtypeStruct(stat, F32),
+            pltpu.VMEM((layers, row_dev, blocks_per, quarter), BF16),
+            pltpu.VMEM(stat, F32),
+            pltpu.VMEM(stat, F32),
+            pltpu.VMEM(stat, F32),
         ),
-        in_specs=[hbm] * 7,
-        out_specs=[hbm] * 4,
+        in_specs=[hbm, pl.BlockSpec(memory_space=pl.ANY)] + [hbm] * 5,
+        out_specs=[vmem] * 4,
         scratch_shapes=[
             pltpu.VMEM(owner_slot.shape, I32),
             pltpu.VMEM((4, layers, row_dev, blocks_per, quarter), BF16),
@@ -380,13 +384,11 @@
             pltpu.VMEM(stat, F32),
             pltpu.VMEM(stat, F32),
             pltpu.VMEM(stat, F32),
-            pltpu.VMEM((layers, row_dev, blocks_per, quarter), BF16),
             dma((10,)),
-            dma((6,)),
             dma, dma,
             dma, dma,
             dma, dma,
-            dma, dma((2,)),
+            dma, dma((2,)), dma((2,)),
             dma, dma, dma, dma,
             dma, dma, dma,
             dma, dma((2,)),
@@ -395,17 +397,17 @@
             pltpu.SemaphoreType.REGULAR((5,)),
         ],
         compiler_params=pltpu.CompilerParams(
-            collective_id=0, has_side_effects=True, vmem_limit_bytes=60 << 20
+            collective_id=0, has_side_effects=True, vmem_limit_bytes=40 << 20
         ),
-    )(owner_slot, pieces, stat_left, stat_right, second_moment, basis_left, basis_right)
+    )(stay(owner_slot), pieces, *(stay(a) for a in (stat_left, stat_right, second_moment, basis_left, basis_right)))
     return pl.pallas_call(
         store_kernel,
         name="store",
         out_shape=tuple(jax.ShapeDtypeStruct(r.shape, r.dtype) for r in results),
-        in_specs=[hbm] * 4,
+        in_specs=[vmem] * 4,
         out_specs=[hbm] * 4,
-        scratch_shapes=[pltpu.VMEM(r.shape, r.dtype) for r in results] + [dma((8,))],
-        compiler_params=pltpu.CompilerParams(vmem_limit_bytes=60 << 20),
+        scratch_shapes=[dma((4,))],
+        compiler_params=pltpu.CompilerParams(vmem_limit_bytes=8 << 20),
     )(*results)
 
 

time: 76.8 us -> 68.9 us (0.90)
  Pallas kernels: 73.8 us -> 66.7 us
  local copies, waits for them, and re-layouts: 2.21 us -> 1.42 us
    pallas_call x1, Pallas kernels: 71.5 us -> 65.5 us  [local(): pl.pallas_call(kernel, name='soap_step', out_shape=(pltpu.VMEM((layers, r...]
    pallas_call x1, Pallas kernels: 2.32 us -> 1.22 us  [local(): pl.pallas_call(store_kernel, name='store', out_shape=tuple((jax.ShapeDtyp...]
    reshape x1, local copies, waits for them, and re-layouts: 2.21 us -> 1.42 us  [local(): pieces = gradient.reshape(layers, row_dev, blocks_per, order)]
where the time goes in v3:
time: 68.9 us; the launch traced here: 68.7 us
  Pallas kernels  66.7 us (97%)
  local copies, waits for them, and re-layouts  1.42 us (2%)
    pallas_call x1, Pallas kernels, local(): pl.pallas_call(kernel, name='soap_step', out_shape=(pltpu.VMEM((layers, r...  65.5 us
    reshape x1, local copies, waits for them, and re-layouts, local(): pieces = gradient.reshape(layers, row_dev, blocks_per, order)  1.42 us

profile of v3, /device:TPU:1, one launch (start us, length us, event | category | flops | bytes accessed | tf_op | source)
XLA Modules:
  0.0 68.7 jit_solution(9714601777090114684)
XLA Ops:
  0.6 1.4 %reshape.11.grad_ref = bf16[8,4,16,512]{3,2,1,0:T(8,128)(2,1)S(1)} reshape(bf16[1,8,4,8192]{3,2,1,0:T(4,128)(2,1)} %param.7) | data formatting | bytes 1048576 | tf_op jit(solution)/shard_map/reshape | solution.py:345
  2.0 65.5 %soap_step.1 = (bf16[8,4,16,128]{3,2,1,0:T(8,128)(2,1)S(1)}, f32[2,128,512]{2,1,0:T(8,128)S(1)}, f32[2,128,512]{2,1,0:T(8,128)S(1)}, f32[2,128,512]{2,1,0:T(8,128)S(1)}) custom-call(s32[8,16]{1,0:T(8,128)} %slot_ref.1, bf16[8,4,16,512]{3,2,1,0:T(8,128)(2,1)S(1)} %reshape.11.grad_ref, f32[2,128,512]{2,1,0:T(8,128)} %left_ref.1, f32[2,128,512]{2,1,0:T(8,128)} %right_ref.1, ...), custom_call_target="tpu_custom_call" | custom-call | tf_op jit(solution)/shard_map/soap_step/pallas_call | solution.py:352
  67.5 1.2 %store.1 = (bf16[8,4,16,128]{3,2,1,0:T(8,128)(2,1)}, f32[2,128,512]{2,1,0:T(8,128)}, f32[2,128,512]{2,1,0:T(8,128)}, f32[2,128,512]{2,1,0:T(8,128)}) custom-call(bf16[8,4,16,128]{3,2,1,0:T(8,128)(2,1)S(1)} %get-tuple-element.8.refs_0_, f32[2,128,512]{2,1,0:T(8,128)S(1)} %get-tuple-element.9.refs_1_, f32[2,128,512]{2,1,0:T(8,128)S(1)} %get-tuple-element.10.refs_2_, ...), custom_call_target="tpu_custom_call" | custom-call | tf_op jit(solution)/shard_map/store/pallas_call | solution.py:403

commit v4 on v3

--- a/solution.py
+++ b/solution.py
@@ -43,7 +43,7 @@
     send_b, recv_b, g_full, l_full, r_full, l_own, back_own, back_full,
     out_own, out_sib, send_e, recv_e, stat_l, stat_r, stat_m,
     local_sem, a_send, a_recv, x_send, x_recv, b_send, b_recv, c_send, c_near, c_far,
-    l_send, l_near, l_far, l_last, r_send, r_near, r_far, d_send, d_recv, y_send, y_recv,
+    l_send, l_near, l_far, r_send, r_near, r_far, d_send, d_recv, y_send, y_recv,
     e_send, e_recv, tokens,
 ):
     x = lax.axis_index("dp")
@@ -185,24 +185,27 @@
     arrived(("token", 3))
     greet(4, y_peer)
 
+    arrived("groups sent")
+    for t in range(2):
+        for d in (1, -1):
+            mine = r_full.at[t, column(x), :]
+            remote(mine, mine, r_send, r_near, (x_peer(d), f)).start()
+    for t in range(2):
+        for d in (1, -1):
+            mine = l_full.at[t, :, column(x)]
+            remote(mine, mine, l_send, l_near, (x_peer(d), f)).start()
+    near_rows = pl.ds(0, 2 * quarter)
+    started("right near", r_full.at[:, near_rows, :], r_near)
+    started("right sent", r_full.at[:, near_rows, :], r_send)
+    started("left near", l_full.at[:, near_rows, :], l_near)
+    started("left sent", l_full.at[:, near_rows, :], l_send)
+
     arrived("groups")
     total = raw[0].astype(F32) + raw[1].astype(F32) + raw[2].astype(F32) + raw[3].astype(F32)
     mean[0] = (total * (1.0 / groups)).astype(BF16).reshape(many, LANES)
     share = remote(mean.at[0], mean.at[1], x_send, x_recv, sibling)
     share.start()
     pending["mean"] = share.wait
-    for t in range(2):
-        for d in (1, -1):
-            mine = r_full.at[t, column(x), :]
-            remote(mine, mine, r_send, r_near, (x_peer(d), f)).start()
-    for d in (1, -1):
-        mine = l_full.at[0, :, column(x)]
-        remote(mine, mine, l_send, l_near, (x_peer(d), f)).start()
-    started("right near", r_full.at[:, pl.ds(0, 2 * quarter), :], r_near)
-    started("right sent", r_full.at[:, pl.ds(0, 2 * quarter), :], r_send)
-    started("left near", l_full.at[0, pl.ds(0, 2 * quarter), :], l_near)
-    started("left sent", l_full.at[0, pl.ds(0, 2 * quarter), :], l_send)
-
     near = dot(pick[...], mean[0]).reshape(chips, 2 * rows, LANES)
     arrived("mean")
     away = dot(pick[...], mean[1]).reshape(chips, 2 * rows, LANES)
@@ -231,13 +234,6 @@
     started("right", r_full.at[:, pl.ds(0, quarter), :], r_far)
     started("right sent", r_full.at[:, parts, :], r_send)
 
-    arrived("left near")
-    for i, d in enumerate((1, -1)):
-        piece = l_full.at[0, pl.ds(i * (order // 2), order // 2), column(x_peer(-d))]
-        remote(piece, piece, l_send, l_far, (x_peer(d), f)).start()
-    started("left 0", l_full.at[0, pl.ds(0, quarter), :], l_far)
-    started("left sent", l_full.at[0, parts, :], l_send)
-
     arrived("rows")
     for j in range(chips // per):
         rows_j = dot(sort_in[...], recv_b[j * per : (j + 1) * per].reshape(chunk, LANES)).astype(BF16)
@@ -256,10 +252,12 @@
             remote(piece, piece, c_send, c_far.at[t], (x_peer(d), f)).start()
         started(("block", t), g_full.at[t, pl.ds(0, quarter), :], c_far.at[t])
     started("blocks sent", g_full.at[:, parts, :], c_send)
-    for d in (2, 1, -1):
-        mine = l_full.at[1, :, column(x)]
-        remote(mine, mine, l_send, l_last, (x_peer(d), f)).start()
-    started("left 1", l_full.at[1, parts, :], l_last)
+    arrived("left near")
+    for t in range(2):
+        for i, d in enumerate((1, -1)):
+            piece = l_full.at[t, pl.ds(i * (order // 2), order // 2), column(x_peer(-d))]
+            remote(piece, piece, l_send, l_far, (x_peer(d), f)).start()
+    started("left", l_full.at[:, pl.ds(0, quarter), :], l_far)
     started("left sent", l_full.at[:, parts, :], l_send)
     arrived("right")
 
@@ -293,9 +291,8 @@
     block_step(0)
     arrived(("block", 1))
     block_step(1)
-    arrived("left 0")
+    arrived("left")
     out_step(0)
-    arrived("left 1")
     out_step(1)
     def sort_rows(ref, sort, j):
         both = jnp.concatenate([ref[t, j * part : (j + 1) * part] for t in range(2)], axis=0)
@@ -389,7 +386,7 @@
             dma, dma,
             dma, dma,
             dma, dma((2,)), dma((2,)),
-            dma, dma, dma, dma,
+            dma, dma, dma,
             dma, dma, dma,
             dma, dma((2,)),
             dma, dma((2,)),

time: 68.9 us -> 66 us (0.958)
  Pallas kernels: 66.7 us -> 63.8 us
    pallas_call x1, Pallas kernels: 65.5 us -> 62.6 us  [local(): pl.pallas_call(kernel, name='soap_step', out_shape=(pltpu.VMEM((layers, r...]
where the time goes in v4:
time: 66 us; the launch traced here: 65.9 us
  Pallas kernels  63.8 us (97%)
  local copies, waits for them, and re-layouts  1.42 us (2%)
    pallas_call x1, Pallas kernels, local(): pl.pallas_call(kernel, name='soap_step', out_shape=(pltpu.VMEM((layers, r...  62.6 us
    reshape x1, local copies, waits for them, and re-layouts, local(): pieces = gradient.reshape(layers, row_dev, blocks_per, order)  1.42 us

profile of v4, /device:TPU:1, one launch (start us, length us, event | category | flops | bytes accessed | tf_op | source)
XLA Modules:
  0.0 65.9 jit_solution(15223462445242958423)
XLA Ops:
  0.6 1.4 %reshape.11.grad_ref = bf16[8,4,16,512]{3,2,1,0:T(8,128)(2,1)S(1)} reshape(bf16[1,8,4,8192]{3,2,1,0:T(4,128)(2,1)} %param.7) | data formatting | bytes 1048576 | tf_op jit(solution)/shard_map/reshape | solution.py:342
  2.0 62.6 %soap_step.1 = (bf16[8,4,16,128]{3,2,1,0:T(8,128)(2,1)S(1)}, f32[2,128,512]{2,1,0:T(8,128)S(1)}, f32[2,128,512]{2,1,0:T(8,128)S(1)}, f32[2,128,512]{2,1,0:T(8,128)S(1)}) custom-call(s32[8,16]{1,0:T(8,128)} %slot_ref.1, bf16[8,4,16,512]{3,2,1,0:T(8,128)(2,1)S(1)} %reshape.11.grad_ref, f32[2,128,512]{2,1,0:T(8,128)} %left_ref.1, f32[2,128,512]{2,1,0:T(8,128)} %right_ref.1, ...), custom_call_target="tpu_custom_call" | custom-call | tf_op jit(solution)/shard_map/soap_step/pallas_call | solution.py:349
  64.6 1.2 %store.1 = (bf16[8,4,16,128]{3,2,1,0:T(8,128)(2,1)}, f32[2,128,512]{2,1,0:T(8,128)}, f32[2,128,512]{2,1,0:T(8,128)}, f32[2,128,512]{2,1,0:T(8,128)}) custom-call(bf16[8,4,16,128]{3,2,1,0:T(8,128)(2,1)S(1)} %get-tuple-element.8.refs_0_, f32[2,128,512]{2,1,0:T(8,128)S(1)} %get-tuple-element.9.refs_1_, f32[2,128,512]{2,1,0:T(8,128)S(1)} %get-tuple-element.10.refs_2_, ...), custom_call_target="tpu_custom_call" | custom-call | tf_op jit(solution)/shard_map/store/pallas_call | solution.py:400

commit v5 on v4

--- a/solution.py
+++ b/solution.py
@@ -39,8 +39,8 @@
 def kernel(
     slot_ref, grad_ref, left_ref, right_ref, moment_ref, bl_ref, br_ref,
     update_ref, new_left_ref, new_right_ref, new_moment_ref,
-    slot_vmem, raw, mean, pick, place, sort_in, sort_own, sort_sib,
-    send_b, recv_b, g_full, l_full, r_full, l_own, back_own, back_full,
+    slot_vmem, grad, parted, raw, mean, pick, place, sort_in, sort_own, sort_sib,
+    send_b, recv_b, g_full, l_full, r_full, l_own, l_turned, rotated_ref, back_own, back_full,
     out_own, out_sib, send_e, recv_e, stat_l, stat_r, stat_m,
     local_sem, a_send, a_recv, x_send, x_recv, b_send, b_recv, c_send, c_near, c_far,
     l_send, l_near, l_far, r_send, r_near, r_far, d_send, d_recv, y_send, y_recv,
@@ -54,9 +54,10 @@
     z, y = chip // LINE, lax.rem(chip, LINE)
     chips = LINE * LINE
     sibling = (x, f + 1 - 2 * core)
-    layers, rows, blocks_per, _ = grad_ref.shape
+    layers, rows, columns = grad_ref.shape
+    order = g_full.shape[1]
+    blocks_per = columns // order
     many = layers * rows * blocks_per
-    order = g_full.shape[1]
     quarter = order // groups
     half = quarter // 2
     parts = pl.ds(0, order - quarter)
@@ -110,7 +111,7 @@
 
     loads = [
         pltpu.make_async_copy(slot_ref, slot_vmem, local_sem.at[0]),
-        pltpu.make_async_copy(grad_ref.at[:, :, :, column(x)], raw.at[3], local_sem.at[1]),
+        pltpu.make_async_copy(grad_ref, grad, local_sem.at[1]),
         pltpu.make_async_copy(bl_ref, l_own, local_sem.at[2]),
         pltpu.make_async_copy(left_ref, stat_l, local_sem.at[3]),
         pltpu.make_async_copy(right_ref, stat_r, local_sem.at[4]),
@@ -119,17 +120,39 @@
     for t in range(2):
         loads.append(pltpu.make_async_copy(bl_ref.at[t], l_full.at[t, :, column(x)], local_sem.at[6 + t]))
         loads.append(pltpu.make_async_copy(br_ref.at[t], r_full.at[t, column(x), :], local_sem.at[8 + t]))
+    loads[1].start()
     for i, load in enumerate(loads):
-        load.start()
+        if i != 1:
+            load.start()
         pending["load", i] = load.wait
+    def cut(at, d, h):
+        p = x_peer(d)
+        for l in range(h * some, (h + 1) * some):
+            pieces = [
+                grad[l, :, pl.ds(pl.multiple_of(c * order + p * LANES, LANES), LANES)].astype(F32)
+                for c in range(blocks_per)
+            ]
+            size = rows * blocks_per
+            parted[at, l * size : (l + 1) * size] = jnp.concatenate(pieces, axis=0).astype(BF16)
+
+    some = layers // 2
+    peers = ((1, 2), (0, 1), (2, -1))
+    arrived(("load", 1))
+    cut(*peers[0], 0)
     pl.semaphore_wait(barrier, 8)
 
-    for d in (2, 1, -1):
-        p = x_peer(d)
-        at = {2: 1, 1: 0, -1: 2}[d]
-        remote(grad_ref.at[:, :, :, column(p)], raw.at[at], a_send, a_recv, (p, f)).start()
-    started("groups", raw.at[pl.ds(0, 3)], a_recv)
+    for h in range(2):
+        held = pl.ds(h * (many // 2), many // 2)
+        for at, d in peers:
+            if (at, h) != (peers[0][0], 0):
+                cut(at, d, h)
+            remote(
+                parted.at[at, held], raw.at[at, held], a_send, a_recv.at[h], (x_peer(d), f)
+            ).start()
+        started(("groups", h), raw.at[pl.ds(0, 3), held], a_recv.at[h])
     started("groups sent", raw.at[pl.ds(0, 3)], a_send)
+    for h in range(2):
+        cut(3, 0, h)
 
     def greet(i, peers):
         for d in (1, -1):
@@ -140,11 +163,11 @@
 
     arrived(("load", 0))
     slots = slot_vmem[...].astype(F32).astype(BF16)
-    spread = one_hot(lax.rem(iota((blocks_per, many), 1), blocks_per), iota((blocks_per, many), 0))
+    spread = one_hot(lax.rem(iota((blocks_per, many), 1) // rows, blocks_per), iota((blocks_per, many), 0))
     wide = dot(slots, spread)
     own_layer = iota((layers, many), 1) // (rows * blocks_per) == iota((layers, many), 0)
     slot_lane = jnp.sum(jnp.where(own_layer, wide, 0.0), axis=0, keepdims=True).astype(I32)
-    row_lane = lax.rem(iota((1, many), 1) // blocks_per, rows)
+    row_lane = lax.rem(iota((1, many), 1), rows)
     owner_lane = slot_lane // 2
     code_lane = jnp.where(
         lax.rem(owner_lane, 2) == core,
@@ -180,11 +203,25 @@
     sort_sib[...] = one_hot(jnp.where(far_o == 1, want, -1), co)
     arrived(("token", 2))
     greet(3, y_peer)
-    for i in range(1, len(loads)):
+    for i in range(2, len(loads)):
         arrived(("load", i))
+    for t in range(2):
+        l_turned[t] = l_own[t].astype(F32).T.astype(BF16)
     arrived(("token", 3))
     greet(4, y_peer)
 
+    def add_groups(h):
+        arrived(("groups", h))
+        lines = pl.ds(h * (many // 2), many // 2)
+        total = parted[3, lines].astype(F32)
+        for g in range(groups - 1):
+            total = total + raw[g, lines].astype(F32)
+        mean[0, lines] = (total * (1.0 / groups)).astype(BF16)
+        remote(mean.at[0, lines], mean.at[1, lines], x_send, x_recv.at[h], sibling).start()
+        started(("mean", h), mean.at[1, lines], x_recv.at[h])
+        started("mean sent", mean.at[0, pl.ds(0, (h + 1) * (many // 2))], x_send)
+
+    add_groups(0)
     arrived("groups sent")
     for t in range(2):
         for d in (1, -1):
@@ -200,23 +237,18 @@
     started("left near", l_full.at[:, near_rows, :], l_near)
     started("left sent", l_full.at[:, near_rows, :], l_send)
 
-    arrived("groups")
-    total = raw[0].astype(F32) + raw[1].astype(F32) + raw[2].astype(F32) + raw[3].astype(F32)
-    mean[0] = (total * (1.0 / groups)).astype(BF16).reshape(many, LANES)
-    share = remote(mean.at[0], mean.at[1], x_send, x_recv, sibling)
-    share.start()
-    pending["mean"] = share.wait
-    near = dot(pick[...], mean[0]).reshape(chips, 2 * rows, LANES)
-    arrived("mean")
-    away = dot(pick[...], mean[1]).reshape(chips, 2 * rows, LANES)
-    send_b[...] = jnp.concatenate([near, away], axis=1).astype(BF16)
+    add_groups(1)
+    arrived(("mean", 0))
+    arrived(("mean", 1))
 
     arrived(("token", 4))
 
     along_z = [lax.rem(z + d, LINE) for d in range(LINE)]
     along_y = [lax.rem(y + d, LINE) for d in range(LINE)]
 
-    def all_to_all(name, src, dst, send, recv):
+    def all_to_all(name, fill, src, dst, send, recv):
+        for k in range(LINE // 2):
+            fill(k, lax.rem(z // 2 + k, LINE // 2))
         for dz, dy in far_first:
             to = along_z[dz] * LINE + along_y[dy]
             remote(src.at[to], dst.at[chip], send, recv, (x, to * 2 + core)).start()
@@ -224,7 +256,14 @@
         started(name, dst.at[pl.ds(0, chips - 1)], recv)
         started(name + " sent", src.at[pl.ds(0, chips - 1)], send)
 
-    all_to_all("rows", send_b, recv_b, b_send, b_recv)
+    def fill_rows(k, j):
+        lines = pl.ds(pl.multiple_of(j * part, part), part)
+        near, away = (
+            dot(pick[lines, :], mean[i]).reshape(per, 2 * rows, LANES) for i in range(2)
+        )
+        send_b[pl.ds(j * per, per)] = jnp.concatenate([near, away], axis=1).astype(BF16)
+
+    all_to_all("rows", fill_rows, send_b, recv_b, b_send, b_recv)
 
     arrived("right near")
     for t in range(2):
@@ -261,11 +300,19 @@
     started("left sent", l_full.at[:, parts, :], l_send)
     arrived("right")
 
+    def turn(t, pieces):
+        total = 0.0
+        for p in pieces:
+            half_turn = dot(l_turned[t], g_full[t, :, column(p)]).astype(BF16)
+            total = total + dot(half_turn, r_full[t, column(p), :])
+        return total
+
+    for t in range(2):
+        rotated_ref[t] = turn(t, (x, x_peer(1), x_peer(-1)))
+
     def block_step(t):
-        block = g_full[t]
+        rotated = rotated_ref[t] + turn(t, (x_peer(2),))
         right = r_full[t]
-        half_turn = dot(l_own[t], block, 0, 0).astype(BF16)
-        rotated = dot(half_turn, right)
         moment = 0.95 * stat_m[t] + 0.05 * rotated * rotated
         new_moment_ref[t] = jnp.where(used[t] > 0.0, moment, stat_m[t])
         scaled = (rotated / (jnp.sqrt(moment) + epsilon)).astype(BF16)
@@ -295,17 +342,19 @@
     out_step(0)
     out_step(1)
     def sort_rows(ref, sort, j):
-        both = jnp.concatenate([ref[t, j * part : (j + 1) * part] for t in range(2)], axis=0)
+        lines = pl.ds(pl.multiple_of(j * part, part), part)
+        both = jnp.concatenate([ref[t, lines, :] for t in range(2)], axis=0)
         return dot(sort[...], both)
 
-    mine = [sort_rows(out_own, sort_own, j) for j in range(chips // per)]
+    mine = [sort_rows(out_own, sort_own, lax.rem(z // 2 + k, LINE // 2)) for k in range(LINE // 2)]
     arrived(("out", 0))
     arrived(("out", 1))
-    for j in range(chips // per):
-        both = (mine[j] + sort_rows(out_sib, sort_sib, j)).astype(BF16)
-        send_e[j * per : (j + 1) * per] = both.reshape(per, 4 * rows, LANES)
-
-    all_to_all("update", send_e, recv_e, e_send, e_recv)
+
+    def fill_update(k, j):
+        both = (mine[k] + sort_rows(out_sib, sort_sib, j)).astype(BF16)
+        send_e[pl.ds(j * per, per)] = both.reshape(per, 4 * rows, LANES)
+
+    all_to_all("update", fill_update, send_e, recv_e, e_send, e_recv)
     for t in range(2):
         block = g_full[t]
         left_term = dot(g_full[t, column(x), :], block, 1, 1)
@@ -339,7 +388,6 @@
     blocks_per = columns // order
     chips = LINE * LINE
     many = layers * blocks_per * row_dev
-    pieces = gradient.reshape(layers, row_dev, blocks_per, order)
     vmem = pl.BlockSpec(memory_space=pltpu.VMEM)
     hbm = pl.BlockSpec(memory_space=pltpu.HBM)
     dma = pltpu.SemaphoreType.DMA
@@ -355,11 +403,13 @@
             pltpu.VMEM(stat, F32),
             pltpu.VMEM(stat, F32),
         ),
-        in_specs=[hbm, pl.BlockSpec(memory_space=pl.ANY)] + [hbm] * 5,
+        in_specs=[hbm] * 7,
         out_specs=[vmem] * 4,
         scratch_shapes=[
             pltpu.VMEM(owner_slot.shape, I32),
-            pltpu.VMEM((4, layers, row_dev, blocks_per, quarter), BF16),
+            pltpu.VMEM(gradient.shape[1:], BF16),
+            pltpu.VMEM((4, many, quarter), BF16),
+            pltpu.VMEM((3, many, quarter), BF16),
             pltpu.VMEM((2, many, quarter), BF16),
             pltpu.VMEM((chips * 2 * row_dev, many), BF16),
             pltpu.VMEM((many, chips * 4 * row_dev), BF16),
@@ -373,6 +423,8 @@
             pltpu.VMEM(full, BF16),
             pltpu.VMEM((capacity, order, quarter), BF16),
             pltpu.VMEM((capacity, quarter, order), BF16),
+            pltpu.VMEM(stat, F32),
+            pltpu.VMEM((capacity, quarter, order), BF16),
             pltpu.VMEM((capacity, order, quarter), BF16),
             pltpu.VMEM((capacity, order, quarter), BF16),
             pltpu.VMEM((capacity, order, quarter), BF16),
@@ -382,8 +434,8 @@
             pltpu.VMEM(stat, F32),
             pltpu.VMEM(stat, F32),
             dma((10,)),
-            dma, dma,
-            dma, dma,
+            dma, dma((2,)),
+            dma, dma((2,)),
             dma, dma,
             dma, dma((2,)), dma((2,)),
             dma, dma, dma,
@@ -396,7 +448,7 @@
         compiler_params=pltpu.CompilerParams(
             collective_id=0, has_side_effects=True, vmem_limit_bytes=40 << 20
         ),
-    )(stay(owner_slot), pieces, *(stay(a) for a in (stat_left, stat_right, second_moment, basis_left, basis_right)))
+    )(*(stay(a) for a in (owner_slot, gradient[0], stat_left, stat_right, second_moment, basis_left, basis_right)))
     return pl.pallas_call(
         store_kernel,
         name="store",

time: 66 us -> 64.9 us (0.983)
  local copies, waits for them, and re-layouts: 1.42 us -> 0 us
    reshape x1 -> x0, local copies, waits for them, and re-layouts: 1.42 us -> none  [local(): pieces = gradient.reshape(layers, row_dev, blocks_per, order)]
where the time goes in v5:
time: 64.9 us; the launch traced here: 64.8 us
  Pallas kernels  64.2 us (99%)
    pallas_call x1, Pallas kernels, local(): pl.pallas_call(kernel, name='soap_step', out_shape=(pltpu.VMEM((layers, r...  62.9 us

profile of v5, /device:TPU:1, one launch (start us, length us, event | category | flops | bytes accessed | tf_op | source)
XLA Modules:
  0.0 64.8 jit_solution(4704387521747764402)
XLA Ops:
  0.6 62.9 %soap_step.1 = (bf16[8,4,16,128]{3,2,1,0:T(8,128)(2,1)S(1)}, f32[2,128,512]{2,1,0:T(8,128)S(1)}, f32[2,128,512]{2,1,0:T(8,128)S(1)}, f32[2,128,512]{2,1,0:T(8,128)S(1)}) custom-call(s32[8,16]{1,0:T(8,128)} %slot_ref.1, bf16[8,4,8192]{2,1,0:T(4,128)(2,1)} %bitcast.1, f32[2,128,512]{2,1,0:T(8,128)} %left_ref.1, f32[2,128,512]{2,1,0:T(8,128)} %right_ref.1, ...), custom_call_target="tpu_custom_call" | custom-call | tf_op jit(solution)/shard_map/soap_step/pallas_call | solution.py:397
  63.6 1.2 %store.1 = (bf16[8,4,16,128]{3,2,1,0:T(8,128)(2,1)}, f32[2,128,512]{2,1,0:T(8,128)}, f32[2,128,512]{2,1,0:T(8,128)}, f32[2,128,512]{2,1,0:T(8,128)}) custom-call(bf16[8,4,16,128]{3,2,1,0:T(8,128)(2,1)S(1)} %get-tuple-element.8.refs_0_, f32[2,128,512]{2,1,0:T(8,128)S(1)} %get-tuple-element.9.refs_1_, f32[2,128,512]{2,1,0:T(8,128)S(1)} %get-tuple-element.10.refs_2_, ...), custom_call_target="tpu_custom_call" | custom-call | tf_op jit(solution)/shard_map/store/pallas_call | solution.py:452

commit v6 on v5

--- a/solution.py
+++ b/solution.py
@@ -153,6 +153,16 @@
     started("groups sent", raw.at[pl.ds(0, 3)], a_send)
     for h in range(2):
         cut(3, 0, h)
+
+    for i in range(6, 10):
+        arrived(("load", i))
+    for t in range(2):
+        for d in (1, -1):
+            mine = r_full.at[t, column(x), :]
+            remote(mine, mine, r_send, r_near, (x_peer(d), f)).start()
+    near_rows = pl.ds(0, 2 * quarter)
+    started("right near", r_full.at[:, near_rows, :], r_near)
+    started("right sent", r_full.at[:, near_rows, :], r_send)
 
     def greet(i, peers):
         for d in (1, -1):
@@ -203,7 +213,7 @@
     sort_sib[...] = one_hot(jnp.where(far_o == 1, want, -1), co)
     arrived(("token", 2))
     greet(3, y_peer)
-    for i in range(2, len(loads)):
+    for i in range(2, 6):
         arrived(("load", i))
     for t in range(2):
         l_turned[t] = l_own[t].astype(F32).T.astype(BF16)
@@ -225,15 +235,8 @@
     arrived("groups sent")
     for t in range(2):
         for d in (1, -1):
-            mine = r_full.at[t, column(x), :]
-            remote(mine, mine, r_send, r_near, (x_peer(d), f)).start()
-    for t in range(2):
-        for d in (1, -1):
             mine = l_full.at[t, :, column(x)]
             remote(mine, mine, l_send, l_near, (x_peer(d), f)).start()
-    near_rows = pl.ds(0, 2 * quarter)
-    started("right near", r_full.at[:, near_rows, :], r_near)
-    started("right sent", r_full.at[:, near_rows, :], r_send)
     started("left near", l_full.at[:, near_rows, :], l_near)
     started("left sent", l_full.at[:, near_rows, :], l_send)
 

time: 64.9 us -> 64.1 us (0.988)
  Pallas kernels: 64.2 us -> 63.4 us
    pallas_call x1, Pallas kernels: 62.9 us -> 62.1 us  [local(): pl.pallas_call(kernel, name='soap_step', out_shape=(pltpu.VMEM((layers, r...]
where the time goes in v6:
time: 64.1 us; the launch traced here: 64 us
  Pallas kernels  63.4 us (99%)
    pallas_call x1, Pallas kernels, local(): pl.pallas_call(kernel, name='soap_step', out_shape=(pltpu.VMEM((layers, r...  62.1 us

profile of v6, /device:TPU:1, one launch (start us, length us, event | category | flops | bytes accessed | tf_op | source)
XLA Modules:
  0.0 64.0 jit_solution(5315252400437876653)
XLA Ops:
  0.6 62.1 %soap_step.1 = (bf16[8,4,16,128]{3,2,1,0:T(8,128)(2,1)S(1)}, f32[2,128,512]{2,1,0:T(8,128)S(1)}, f32[2,128,512]{2,1,0:T(8,128)S(1)}, f32[2,128,512]{2,1,0:T(8,128)S(1)}) custom-call(s32[8,16]{1,0:T(8,128)} %slot_ref.1, bf16[8,4,8192]{2,1,0:T(4,128)(2,1)} %bitcast.1, f32[2,128,512]{2,1,0:T(8,128)} %left_ref.1, f32[2,128,512]{2,1,0:T(8,128)} %right_ref.1, ...), custom_call_target="tpu_custom_call" | custom-call | tf_op jit(solution)/shard_map/soap_step/pallas_call | solution.py:400
  62.8 1.2 %store.1 = (bf16[8,4,16,128]{3,2,1,0:T(8,128)(2,1)}, f32[2,128,512]{2,1,0:T(8,128)}, f32[2,128,512]{2,1,0:T(8,128)}, f32[2,128,512]{2,1,0:T(8,128)}) custom-call(bf16[8,4,16,128]{3,2,1,0:T(8,128)(2,1)S(1)} %get-tuple-element.8.refs_0_, f32[2,128,512]{2,1,0:T(8,128)S(1)} %get-tuple-element.9.refs_1_, f32[2,128,512]{2,1,0:T(8,128)S(1)} %get-tuple-element.10.refs_2_, ...), custom_call_target="tpu_custom_call" | custom-call | tf_op jit(solution)/shard_map/store/pallas_call | solution.py:455

commit v7 on v6

--- a/solution.py
+++ b/solution.py
@@ -141,6 +141,13 @@
     cut(*peers[0], 0)
     pl.semaphore_wait(barrier, 8)
 
+    def greet(i, peers):
+        for d in (1, -1):
+            signal(tokens.at[i], peers(d * (2 if i in (1, 4) else 1)))
+        pending["token", i] = lambda: pl.semaphore_wait(tokens.at[i], 2)
+
+    greet(0, z_peer)
+
     for h in range(2):
         held = pl.ds(h * (many // 2), many // 2)
         for at, d in peers:
@@ -163,13 +170,6 @@
     near_rows = pl.ds(0, 2 * quarter)
     started("right near", r_full.at[:, near_rows, :], r_near)
     started("right sent", r_full.at[:, near_rows, :], r_send)
-
-    def greet(i, peers):
-        for d in (1, -1):
-            signal(tokens.at[i], peers(d * (2 if i in (1, 4) else 1)))
-        pending["token", i] = lambda: pl.semaphore_wait(tokens.at[i], 2)
-
-    greet(0, z_peer)
 
     arrived(("load", 0))
     slots = slot_vmem[...].astype(F32).astype(BF16)
@@ -217,8 +217,6 @@
         arrived(("load", i))
     for t in range(2):
         l_turned[t] = l_own[t].astype(F32).T.astype(BF16)
-    arrived(("token", 3))
-    greet(4, y_peer)
 
     def add_groups(h):
         arrived(("groups", h))
@@ -232,6 +230,8 @@
         started("mean sent", mean.at[0, pl.ds(0, (h + 1) * (many // 2))], x_send)
 
     add_groups(0)
+    arrived(("token", 3))
+    greet(4, y_peer)
     arrived("groups sent")
     for t in range(2):
         for d in (1, -1):
@@ -241,6 +241,7 @@
     started("left sent", l_full.at[:, near_rows, :], l_send)
 
     add_groups(1)
+    near = [dot(pick[j * part : (j + 1) * part], mean[0]) for j in range(LINE // 2)]
     arrived(("mean", 0))
     arrived(("mean", 1))
 
@@ -250,8 +251,8 @@
     along_y = [lax.rem(y + d, LINE) for d in range(LINE)]
 
     def all_to_all(name, fill, src, dst, send, recv):
-        for k in range(LINE // 2):
-            fill(k, lax.rem(z // 2 + k, LINE // 2))
+        for j in range(LINE // 2):
+            fill(j)
         for dz, dy in far_first:
             to = along_z[dz] * LINE + along_y[dy]
             remote(src.at[to], dst.at[chip], send, recv, (x, to * 2 + core)).start()
@@ -259,12 +260,10 @@
         started(name, dst.at[pl.ds(0, chips - 1)], recv)
         started(name + " sent", src.at[pl.ds(0, chips - 1)], send)
 
-    def fill_rows(k, j):
-        lines = pl.ds(pl.multiple_of(j * part, part), part)
-        near, away = (
-            dot(pick[lines, :], mean[i]).reshape(per, 2 * rows, LANES) for i in range(2)
-        )
-        send_b[pl.ds(j * per, per)] = jnp.concatenate([near, away], axis=1).astype(BF16)
+    def fill_rows(j):
+        away = dot(pick[j * part : (j + 1) * part], mean[1])
+        both = [v.reshape(per, 2 * rows, LANES) for v in (near[j], away)]
+        send_b[j * per : (j + 1) * per] = jnp.concatenate(both, axis=1).astype(BF16)
 
     all_to_all("rows", fill_rows, send_b, recv_b, b_send, b_recv)
 
@@ -345,17 +344,16 @@
     out_step(0)
     out_step(1)
     def sort_rows(ref, sort, j):
-        lines = pl.ds(pl.multiple_of(j * part, part), part)
-        both = jnp.concatenate([ref[t, lines, :] for t in range(2)], axis=0)
+        both = jnp.concatenate([ref[t, j * part : (j + 1) * part] for t in range(2)], axis=0)
         return dot(sort[...], both)
 
-    mine = [sort_rows(out_own, sort_own, lax.rem(z // 2 + k, LINE // 2)) for k in range(LINE // 2)]
+    mine = [sort_rows(out_own, sort_own, j) for j in range(LINE // 2)]
     arrived(("out", 0))
     arrived(("out", 1))
 
-    def fill_update(k, j):
-        both = (mine[k] + sort_rows(out_sib, sort_sib, j)).astype(BF16)
-        send_e[pl.ds(j * per, per)] = both.reshape(per, 4 * rows, LANES)
+    def fill_update(j):
+        both = (mine[j] + sort_rows(out_sib, sort_sib, j)).astype(BF16)
+        send_e[j * per : (j + 1) * per] = both.reshape(per, 4 * rows, LANES)
 
     all_to_all("update", fill_update, send_e, recv_e, e_send, e_recv)
     for t in range(2):

time: 64.1 us -> 64.2 us (level)
  no operation moved by 1% of the time
where the time goes in v7:
time: 64.2 us; the launch traced here: 64 us
  Pallas kernels  63.4 us (99%)
    pallas_call x1, Pallas kernels, local(): pl.pallas_call(kernel, name='soap_step', out_shape=(pltpu.VMEM((layers, r...  62.2 us

profile of v7, /device:TPU:1, one launch (start us, length us, event | category | flops | bytes accessed | tf_op | source)
XLA Modules:
  0.0 64.0 jit_solution(7518997582295733117)
XLA Ops:
  0.6 62.2 %soap_step.1 = (bf16[8,4,16,128]{3,2,1,0:T(8,128)(2,1)S(1)}, f32[2,128,512]{2,1,0:T(8,128)S(1)}, f32[2,128,512]{2,1,0:T(8,128)S(1)}, f32[2,128,512]{2,1,0:T(8,128)S(1)}) custom-call(s32[8,16]{1,0:T(8,128)} %slot_ref.1, bf16[8,4,8192]{2,1,0:T(4,128)(2,1)} %bitcast.1, f32[2,128,512]{2,1,0:T(8,128)} %left_ref.1, f32[2,128,512]{2,1,0:T(8,128)} %right_ref.1, ...), custom_call_target="tpu_custom_call" | custom-call | tf_op jit(solution)/shard_map/soap_step/pallas_call | solution.py:398
  62.8 1.2 %store.1 = (bf16[8,4,16,128]{3,2,1,0:T(8,128)(2,1)}, f32[2,128,512]{2,1,0:T(8,128)}, f32[2,128,512]{2,1,0:T(8,128)}, f32[2,128,512]{2,1,0:T(8,128)}) custom-call(bf16[8,4,16,128]{3,2,1,0:T(8,128)(2,1)S(1)} %get-tuple-element.8.refs_0_, f32[2,128,512]{2,1,0:T(8,128)S(1)} %get-tuple-element.9.refs_1_, f32[2,128,512]{2,1,0:T(8,128)S(1)} %get-tuple-element.10.refs_2_, ...), custom_call_target="tpu_custom_call" | custom-call | tf_op jit(solution)/shard_map/store/pallas_call | solution.py:453

commit v8 on v7

--- a/solution.py
+++ b/solution.py
@@ -38,10 +38,10 @@
 
 def kernel(
     slot_ref, grad_ref, left_ref, right_ref, moment_ref, bl_ref, br_ref,
-    update_ref, new_left_ref, new_right_ref, new_moment_ref,
-    slot_vmem, grad, parted, raw, mean, pick, place, sort_in, sort_own, sort_sib,
+    recv_e, place, new_left_ref, new_right_ref, new_moment_ref,
+    slot_vmem, grad, parted, raw, mean, pick, sort_in, sort_own, sort_sib,
     send_b, recv_b, g_full, l_full, r_full, l_own, l_turned, rotated_ref, back_own, back_full,
-    out_own, out_sib, send_e, recv_e, stat_l, stat_r, stat_m,
+    out_own, out_sib, send_e, stat_l, stat_r, stat_m,
     local_sem, a_send, a_recv, x_send, x_recv, b_send, b_recv, c_send, c_near, c_far,
     l_send, l_near, l_far, r_send, r_near, r_far, d_send, d_recv, y_send, y_recv,
     e_send, e_recv, tokens,
@@ -363,8 +363,6 @@
         right_term = dot(g_full[t, :, column(x)], block, 0, 0)
         new_right_ref[t] = jnp.where(used[t] > 0.0, 0.95 * stat_r[t] + 0.05 * right_term, stat_r[t])
     arrived("update")
-    picked = dot(place[...], recv_e[...].reshape(chips * 4 * rows, LANES))
-    update_ref[...] = picked.astype(BF16).reshape(layers, rows, blocks_per, LANES)
     finish()
 
 
@@ -372,13 +370,20 @@
     return pltpu.with_memory_space_constraint(array, pltpu.HBM)
 
 
-def store_kernel(*refs):
-    count = (len(refs) - 1) // 2
+def store_kernel(
+    rows_ref, place_ref, left_ref, right_ref, moment_ref,
+    update_ref, new_left_ref, new_right_ref, new_moment_ref, update, semaphores,
+):
+    pairs = ((left_ref, new_left_ref), (right_ref, new_right_ref), (moment_ref, new_moment_ref))
     copies = [
-        pltpu.make_async_copy(refs[i], refs[count + i], refs[-1].at[i]) for i in range(count)
+        pltpu.make_async_copy(src, dst, semaphores.at[i]) for i, (src, dst) in enumerate(pairs)
     ]
     for copy in copies:
         copy.start()
+    picked = dot(place_ref[...], rows_ref[...].reshape(place_ref.shape[1], LANES))
+    update[...] = picked.astype(BF16).reshape(update.shape)
+    copies.append(pltpu.make_async_copy(update, update_ref, semaphores.at[3]))
+    copies[3].start()
     for copy in copies:
         copy.wait()
 
@@ -399,13 +404,14 @@
         kernel,
         name="soap_step",
         out_shape=(
-            pltpu.VMEM((layers, row_dev, blocks_per, quarter), BF16),
+            pltpu.VMEM(message, BF16),
+            pltpu.VMEM((many, chips * 4 * row_dev), BF16),
             pltpu.VMEM(stat, F32),
             pltpu.VMEM(stat, F32),
             pltpu.VMEM(stat, F32),
         ),
         in_specs=[hbm] * 7,
-        out_specs=[vmem] * 4,
+        out_specs=[vmem] * 5,
         scratch_shapes=[
             pltpu.VMEM(owner_slot.shape, I32),
             pltpu.VMEM(gradient.shape[1:], BF16),
@@ -413,7 +419,6 @@
             pltpu.VMEM((3, many, quarter), BF16),
             pltpu.VMEM((2, many, quarter), BF16),
             pltpu.VMEM((chips * 2 * row_dev, many), BF16),
-            pltpu.VMEM((many, chips * 4 * row_dev), BF16),
             pltpu.VMEM((256, 256), BF16),
             pltpu.VMEM((256, 256), BF16),
             pltpu.VMEM((256, 256), BF16),
@@ -429,7 +434,6 @@
             pltpu.VMEM((capacity, order, quarter), BF16),
             pltpu.VMEM((capacity, order, quarter), BF16),
             pltpu.VMEM((capacity, order, quarter), BF16),
-            pltpu.VMEM(message, BF16),
             pltpu.VMEM(message, BF16),
             pltpu.VMEM(stat, F32),
             pltpu.VMEM(stat, F32),
@@ -453,10 +457,16 @@
     return pl.pallas_call(
         store_kernel,
         name="store",
-        out_shape=tuple(jax.ShapeDtypeStruct(r.shape, r.dtype) for r in results),
-        in_specs=[vmem] * 4,
+        out_shape=(
+            jax.ShapeDtypeStruct((layers, row_dev, blocks_per, quarter), BF16),
+            *(jax.ShapeDtypeStruct(stat, F32) for _ in range(3)),
+        ),
+        in_specs=[vmem] * 5,
         out_specs=[hbm] * 4,
-        scratch_shapes=[dma((4,))],
+        scratch_shapes=[
+            pltpu.VMEM((layers, row_dev, blocks_per, quarter), BF16),
+            dma((4,)),
+        ],
         compiler_params=pltpu.CompilerParams(vmem_limit_bytes=8 << 20),
     )(*results)
 

time: 64.2 us -> 63.6 us (level)
  no operation moved by 1% of the time
where the time goes in v8:
time: 63.6 us; the launch traced here: 63.5 us
  Pallas kernels  62.8 us (99%)
  between operations  0.64 us (1%)
    pallas_call x1, Pallas kernels, local(): pl.pallas_call(kernel, name='soap_step', out_shape=(pltpu.VMEM(message, B...  61.6 us

profile of v8, /device:TPU:1, one launch (start us, length us, event | category | flops | bytes accessed | tf_op | source)
XLA Modules:
  0.0 63.5 jit_solution(2874863690678297499)
XLA Ops:
  0.6 61.6 %soap_step.1 = (bf16[64,16,128]{2,1,0:T(8,128)(2,1)S(1)}, bf16[512,1024]{1,0:T(8,128)(2,1)S(1)}, f32[2,128,512]{2,1,0:T(8,128)S(1)}, f32[2,128,512]{2,1,0:T(8,128)S(1)}, f32[2,128,512]{2,1,0:T(8,128)S(1)}) custom-call(s32[8,16]{1,0:T(8,128)} %slot_ref.1, bf16[8,4,8192]{2,1,0:T(4,128)(2,1)} %bitcast.1, f32[2,128,512]{2,1,0:T(8,128)} %left_ref.1, ...), custom_call_target="tpu_custom_call" | custom-call | tf_op jit(solution)/shard_map/soap_step/pallas_call | solution.py:403
  62.2 1.2 %store.1 = (bf16[8,4,16,128]{3,2,1,0:T(8,128)(2,1)}, f32[2,128,512]{2,1,0:T(8,128)}, f32[2,128,512]{2,1,0:T(8,128)}, f32[2,128,512]{2,1,0:T(8,128)}) custom-call(bf16[64,16,128]{2,1,0:T(8,128)(2,1)S(1)} %get-tuple-element.9.rows_ref, bf16[512,1024]{1,0:T(8,128)(2,1)S(1)} %get-tuple-element.10.place_ref, f32[2,128,512]{2,1,0:T(8,128)S(1)} %get-tuple-element.11.left_ref, ...), custom_call_target="tpu_custom_call" | custom-call | tf_op jit(solution)/shard_map/store/pallas_call | solution.py:457

commit v9 on v8

--- a/solution.py
+++ b/solution.py
@@ -276,11 +276,11 @@
     started("right sent", r_full.at[:, parts, :], r_send)
 
     arrived("rows")
-    for j in range(chips // per):
-        rows_j = dot(sort_in[...], recv_b[j * per : (j + 1) * per].reshape(chunk, LANES)).astype(BF16)
-        for t in range(2):
-            g_full[t, j * part : (j + 1) * part, column(x)] = rows_j[t * part : (t + 1) * part]
-    for t in range(2):
+    for t in range(2):
+        for j in range(chips // per):
+            rows_j = recv_b[j * per : (j + 1) * per].reshape(chunk, LANES)
+            sorted_j = dot(sort_in[t * part : (t + 1) * part], rows_j)
+            g_full[t, j * part : (j + 1) * part, column(x)] = sorted_j.astype(BF16)
         for d in (1, -1):
             mine = g_full.at[t, :, column(x)]
             remote(mine, mine, c_send, c_near.at[t], (x_peer(d), f)).start()

time: 63.6 us -> 63.5 us (level)
  no operation moved by 1% of the time
where the time goes in v9:
time: 63.5 us; the launch traced here: 63.3 us
  Pallas kernels  62.7 us (99%)
  between operations  0.64 us (1%)
    pallas_call x1, Pallas kernels, local(): pl.pallas_call(kernel, name='soap_step', out_shape=(pltpu.VMEM(message, B...  61.5 us

profile of v9, /device:TPU:1, one launch (start us, length us, event | category | flops | bytes accessed | tf_op | source)
XLA Modules:
  0.0 63.3 jit_solution(2238906966045917224)
XLA Ops:
  0.6 61.5 %soap_step.1 = (bf16[64,16,128]{2,1,0:T(8,128)(2,1)S(1)}, bf16[512,1024]{1,0:T(8,128)(2,1)S(1)}, f32[2,128,512]{2,1,0:T(8,128)S(1)}, f32[2,128,512]{2,1,0:T(8,128)S(1)}, f32[2,128,512]{2,1,0:T(8,128)S(1)}) custom-call(s32[8,16]{1,0:T(8,128)} %slot_ref.1, bf16[8,4,8192]{2,1,0:T(4,128)(2,1)} %bitcast.1, f32[2,128,512]{2,1,0:T(8,128)} %left_ref.1, ...), custom_call_target="tpu_custom_call" | custom-call | tf_op jit(solution)/shard_map/soap_step/pallas_call | solution.py:403
  62.1 1.2 %store.1 = (bf16[8,4,16,128]{3,2,1,0:T(8,128)(2,1)}, f32[2,128,512]{2,1,0:T(8,128)}, f32[2,128,512]{2,1,0:T(8,128)}, f32[2,128,512]{2,1,0:T(8,128)}) custom-call(bf16[64,16,128]{2,1,0:T(8,128)(2,1)S(1)} %get-tuple-element.9.rows_ref, bf16[512,1024]{1,0:T(8,128)(2,1)S(1)} %get-tuple-element.10.place_ref, f32[2,128,512]{2,1,0:T(8,128)S(1)} %get-tuple-element.11.left_ref, ...), custom_call_target="tpu_custom_call" | custom-call | tf_op jit(solution)/shard_map/store/pallas_call | solution.py:457
